TPU v7x, 256 devices: a whole 4x4x8 slice. The times are simulated.
256 devices in a mesh: lat: 32 (over y, x, core), lev: 8 (over z).
Axes of the slice: x: 4, y: 4, z: 8, core: 2. Of those that a mesh axis runs over, the one named last changes fastest.
Arguments:
- innovation: float32 [8, 1280, 2560], P('lev', 'lat'), may hold values from -6 to 6
- obs_mask: int32 [8, 1280, 2560], P('lev', 'lat'), may hold values 0 or 1
- obs_weight: float32 [8, 1280, 2560], P('lev', 'lat'), may hold values from 0.25 to 4
- order: int32 [1280], replicated, may hold values from 0 to 1279, each once
- basis: bfloat16 [1280, 640, 1280], P(('lat', 'lev')), may hold values from -0.15625 to 0.15625
- spread: float32 [8, 1280], replicated, may hold values from 0.25 to 2.5
Outputs:
- control: float32 [1280, 16, 1280], P(('lat', 'lev'))
- increment: float32 [8, 1280, 2560], P('lev', 'lat')
Inputs may be any that keep to these rules, and one draw needn't show every extreme that they name: order holds every wavenumber once.
All inputs are finite; a program needn't handle non-finite values. No bound on the sum of `obs_mask` on one device may be relied on, other than what follows from the above.
Results may differ from a plain program's by a relative error of at most 0.02.
Values may be sent and summed in bfloat16 or wider, within the bound.
No kernel may reach another device: no remote copies, remote signals or barrier semaphores. Data moves between devices by JAX's collectives and lax.ppermute only.
A program may use at most 128 MiB of HBM per device.

v0:
```python
import math

import jax
import jax.numpy as jnp
from jax import lax
from jax.sharding import PartitionSpec as P

ITERS = 2


def wave_table(wavenumbers, points):
    longitude = jnp.arange(points, dtype=jnp.int32)
    phase = longitude[:, None] * wavenumbers[None, :] % points
    angle = phase.astype(jnp.float32) * jnp.float32(2.0 * math.pi / points)
    factor = jnp.float32(math.sqrt(2.0 / points))
    return (
        (jnp.stack([jnp.cos(angle), jnp.sin(angle)], axis=2) * factor)
        .reshape(points, 2 * wavenumbers.shape[0])
        .astype(jnp.bfloat16)
    )


def split_parts(values):
    high_part = values.astype(jnp.bfloat16)
    low_part = (values - high_part.astype(jnp.float32)).astype(jnp.bfloat16)
    return (high_part, low_part)


def parity(wavenumbers, degrees):
    degree = jnp.arange(degrees, dtype=jnp.int32)
    offset = degree[None, :] - wavenumbers[:, None]
    return jnp.where(offset >= 0, jnp.where(offset % 2 == 0, 1.0, -1.0), 0.0).astype(jnp.float32)


def to_owners(fourier):
    return lax.all_to_all(
        lax.all_to_all(fourier, "lat", split_axis=2, concat_axis=1, tiled=True),
        "lev",
        split_axis=2,
        concat_axis=0,
        tiled=True,
    )


def to_bands(fourier):
    sectioned = lax.all_to_all(fourier, "lev", split_axis=0, concat_axis=2, tiled=True)
    return lax.all_to_all(sectioned, "lat", split_axis=1, concat_axis=2, tiled=True)


def squares(residual):
    return lax.psum(jnp.sum(residual * residual), ("lat", "lev"))


def local(innovation, obs_mask, obs_weight, order, basis, spread):
    lev_count = lax.axis_size("lev")
    owned_count = basis.shape[0]
    half_rows = basis.shape[1]
    degrees = basis.shape[2]
    waves_all = order.shape[0]
    levels = spread.shape[0]
    levels_dev = innovation.shape[0]
    lat_rows = innovation.shape[1]
    points = innovation.shape[2]
    owner_index = lax.axis_index("lat") * lev_count + lax.axis_index("lev")
    my_waves = lax.dynamic_slice_in_dim(order, owner_index * owned_count, owned_count)
    wave = wave_table(order, points)
    parity_sign = parity(my_waves, degrees)
    live_mask = jnp.abs(parity_sign)
    spread_rows = jnp.tile(spread, (2, 1))
    obs_scale = obs_mask.astype(jnp.float32) * obs_weight
    zero_value = jnp.zeros((), jnp.bfloat16)

    def synthesis(control):
        scaled = (control * spread_rows[None] * live_mask[:, None, :]).astype(jnp.bfloat16)
        scaled = scaled.reshape(owned_count, 2, levels, degrees)
        even_part = jnp.where(parity_sign[:, None, None, :] > 0, scaled, zero_value)
        odd_part = jnp.where(parity_sign[:, None, None, :] < 0, scaled, zero_value)
        both_parts = jnp.stack([even_part, odd_part], axis=1)
        both_sums = jnp.einsum(
            "sjn,sprln->pljsr", basis, both_parts, preferred_element_type=jnp.float32
        )
        even_sum = both_sums[0]
        odd_sum = both_sums[1]
        fourier = jnp.concatenate([even_sum + odd_sum, (even_sum - odd_sum)[:, ::-1]], axis=1)
        fourier = fourier.reshape(levels, 2 * half_rows, 2 * owned_count).astype(jnp.bfloat16)
        band_rows = to_bands(fourier)
        flat_rows = band_rows.reshape(levels_dev * lat_rows, 2 * waves_all)
        grid_field = jnp.dot(flat_rows, wave.T, preferred_element_type=jnp.float32)
        return grid_field.reshape(levels_dev, lat_rows, points)

    def analysis(grid_field):
        row_count = levels_dev * lat_rows
        grid_hi, grid_lo = split_parts(grid_field.reshape(row_count, points))
        stacked = jnp.concatenate([grid_hi, grid_lo], axis=0)
        product = jnp.dot(stacked, wave, preferred_element_type=jnp.float32)
        fourier = product[:row_count] + product[row_count:]
        fourier = fourier.astype(jnp.bfloat16).reshape(levels_dev, lat_rows, 2 * waves_all)
        owner_rows = to_owners(fourier).reshape(levels, 2 * half_rows, owned_count, 2)
        north_part = owner_rows[:, :half_rows]
        south_part = owner_rows[:, half_rows:][:, ::-1]
        halves = jnp.stack([north_part, south_part], axis=0)
        sums = jnp.einsum("sjn,pljsr->psrln", basis, halves, preferred_element_type=jnp.float32)
        combined = sums[0] * live_mask[:, None, None, :] + parity_sign[:, None, None, :] * sums[1]
        return combined.reshape(owned_count, 2 * levels, degrees) * spread_rows[None]

    rhs = analysis(obs_scale * innovation)
    control = jnp.zeros_like(rhs)
    residual = rhs
    direction = rhs
    norm_now = squares(residual)
    for turn in range(ITERS):
        hessian_out = direction + analysis(obs_scale * synthesis(direction))
        step_size = norm_now / lax.psum(jnp.sum(direction * hessian_out), ("lat", "lev"))
        control = control + step_size * direction
        if turn + 1 < ITERS:
            residual = residual - step_size * hessian_out
            norm_next = squares(residual)
            direction = residual + norm_next / norm_now * direction
            norm_now = norm_next
    increment = synthesis(control)
    return (control, increment)


def solution(mesh):
    in_specs = (
        P("lev", "lat", None),
        P("lev", "lat", None),
        P("lev", "lat", None),
        P(),
        P(("lat", "lev"), None, None),
        P(),
    )
    out_specs = (P(("lat", "lev"), None, None), P("lev", "lat", None))
    return jax.shard_map(local, mesh=mesh, in_specs=in_specs, out_specs=out_specs, check_vma=False)
```

profile of v0, /device:TPU:1, one launch (start us, length us, event | category | flops | bytes accessed | tf_op | source)
XLA Modules:
  0.0 757.4 jit_solution(16213655155876417434)
XLA Ops:
  0.6 53.6 %fusion.6 = (f32[2560,1280,1]{1,0,2:T(8,128)S(1)}, f32[2560,1280,1]{1,0,2:T(8,128)S(1)}) fusion(s32[1280]{0:T(1024)} %param.9), kind=kLoop, calls=%fused_computation.9 | loop fusion | flops 29491200 | bytes 26219520 | tf_op jit(solution)/shard_map/cos | solution.py:17
  60.8 32.8 %copy.181 = bf16[2560,1280,2]{0,2,1:T(2,128)(2,1)} copy(bf16[2560,1280,2]{1,0,2:T(8,128)(2,1)} %fusion) | data formatting | bytes 26214400 | tf_op jit(solution)/shard_map/convert_element_type | solution.py:19
  93.7 27.2 %convert_element_type.137 = bf16[2560,2560]{0,1:T(8,128)(2,1)} reshape(bf16[2560,1280,2]{0,2,1:T(2,128)(2,1)} %copy.181) | data formatting | bytes 26214400 | tf_op jit(solution)/shard_map/convert_element_type | solution.py:19
  121.0 8.8 %fusion.48 = f32[80,2560]{1,0:T(8,128)S(1)} fusion(bf16[2560,2560]{0,1:T(8,128)(2,1)} %convert_element_type.137, bf16[40,2560]{1,0:T(8,128)(2,1)S(1)} %fusion.80, bf16[40,2560]{1,0:T(8,128)(2,1)S(1)} %get-tuple-element.18), kind=kOutput, calls=%fused_computation.48 | convolution fusion | flops 1049395200 | bytes 14336000 | tf_op jit(solution)/shard_map/dot_general | solution.py:95
  131.3 14.3 %reduce.10 = bf16[2560,40]{1,0:T(8,128)(2,1)S(1)} reduce(bf16[2560,1,40]{2,1,0:T(2,128)(2,1)S(1)} %bitcast.302, bf16[]{:T(256)} %broadcast.798), dimensions={1}, to_apply=%bitcast.266.reduce_sub_computation | reduce | bytes 409602
  147.3 8.9 %all-to-all-start = ((bf16[32,2,1600]{2,1,0:T(2,128)(2,1)}), bf16[32,2,1600]{2,1,0:T(2,128)(2,1)S(1)}, u32[]{:S(2)}, u32[]{:S(2)}) async-start(bf16[32,2,1600]{2,1,0:T(2,128)(2,1)} %reshape.540), calls=%async_computation | async-start | bytes 425984 | tf_op jit(solution)/shard_map/all_to_all | solution.py:37
  157.1 7.4 all-to-all-done
  170.0 8.2 %all-to-all-start.1 = ((bf16[8,2,6400]{2,1,0:T(2,128)(2,1)}), bf16[8,2,6400]{2,1,0:T(2,128)(2,1)S(1)}, u32[]{:S(2)}, u32[]{:S(2)}) async-start(bf16[8,2,6400]{2,1,0:T(2,128)(2,1)} %reshape.542), calls=%async_computation.1 | async-start | bytes 409600 | tf_op jit(solution)/shard_map/all_to_all | solution.py:36
  178.3 9.9 %all-to-all-done.1 = bf16[8,2,6400]{2,1,0:T(2,128)(2,1)S(1)} async-done(((bf16[8,2,6400]{2,1,0:T(2,128)(2,1)}), bf16[8,2,6400]{2,1,0:T(2,128)(2,1)S(1)}, u32[]{:S(2)}, u32[]{:S(2)}) %all-to-all-start.1) | async-done | bytes 204832 | tf_op jit(solution)/shard_map/all_to_all | solution.py:36
  201.2 13.3 %all_to_all.198 = bf16[8,1280,10]{1,2,0:T(8,128)(2,1)S(1)} all-to-all(bf16[8,1280,10]{1,2,0:T(8,128)(2,1)S(1)} %copy.194), channel_id=1, replica_groups=mesh['lat'=32,'lev'=8] {'lev'}, dimensions={0} | all-to-all | bytes 409600 | tf_op jit(solution)/shard_map/all_to_all | solution.py:46
  215.1 7.4 reduce.12
  223.2 15.7 %all_to_all.199 = bf16[32,2,1600]{2,1,0:T(2,128)(2,1)S(1)} all-to-all(bf16[32,2,1600]{2,1,0:T(2,128)(2,1)S(1)} %reshape.544), channel_id=1, replica_groups=mesh['lat'=32,'lev'=8] {'lat'}, dimensions={0} | all-to-all | bytes 409600 | tf_op jit(solution)/shard_map/all_to_all | solution.py:47
  239.9 7.1 subtract_convert_fusion.1
  246.9 8.8 %fusion.52 = f32[80,2560]{1,0:T(8,128)S(1)} fusion(bf16[2560,2560]{0,1:T(8,128)(2,1)} %convert_element_type.137, bf16[40,2560]{1,0:T(8,128)(2,1)S(1)} %get-tuple-element.14, bf16[40,2560]{1,0:T(8,128)(2,1)S(1)} %get-tuple-element.15), kind=kOutput, calls=%fused_computation.53 | convolution fusion | flops 1049395200 | bytes 14336000 | tf_op jit(solution)/shard_map/dot_general | solution.py:95
  257.9 15.3 %reduce.13 = bf16[2560,40]{1,0:T(8,128)(2,1)S(1)} reduce(bf16[2560,1,40]{2,1,0:T(2,128)(2,1)} %bitcast.304, bf16[]{:T(256)} %broadcast.798), dimensions={1}, to_apply=%bitcast.272.reduce_sub_computation | reduce | bytes 409602
  274.2 12.2 %all_to_all.200 = bf16[32,2,1600]{2,1,0:T(2,128)(2,1)S(1)} all-to-all(bf16[32,2,1600]{2,1,0:T(2,128)(2,1)S(1)} %reshape.546), channel_id=1, replica_groups=mesh['lat'=32,'lev'=8] {'lat'}, dimensions={0} | all-to-all | bytes 409600 | tf_op jit(solution)/shard_map/all_to_all | solution.py:37
  294.1 13.5 %all_to_all.201 = bf16[8,2,6400]{2,1,0:T(2,128)(2,1)S(1)} all-to-all(bf16[8,2,6400]{2,1,0:T(2,128)(2,1)S(1)} %reshape.548), channel_id=1, replica_groups=mesh['lat'=32,'lev'=8] {'lev'}, dimensions={0} | all-to-all | bytes 409600 | tf_op jit(solution)/shard_map/all_to_all | solution.py:36
  315.0 73.1 %all-reduce = (f32[]{:T(128)}, f32[]{:T(128)}) all-reduce(f32[]{:T(128)} %get-tuple-element.3, f32[]{:T(128)} %get-tuple-element.2), channel_id=1, replica_groups=mesh['lat'=32,'lev'=8] {'lat','lev'}, use_global_device_ids=true, to_apply=%region_1.2 | all-reduce | flops 2 | bytes 16 | tf_op jit(solution)/shard_map/psum | solution.py:51
  390.1 73.5 %psum.30 = f32[]{:T(128)} all-reduce(f32[]{:T(128)} %multiply_reduce_fusion), channel_id=1, replica_groups=mesh['lat'=32,'lev'=8] {'lat','lev'}, use_global_device_ids=true, to_apply=%region_5.6 | all-reduce | flops 1 | bytes 8 | tf_op jit(solution)/shard_map/psum | solution.py:51
  476.9 14.9 %all_to_all.202 = bf16[8,1280,10]{1,2,0:T(8,128)(2,1)} all-to-all(bf16[8,1280,10]{1,2,0:T(8,128)(2,1)S(1)} %copy.208), channel_id=1, replica_groups=mesh['lat'=32,'lev'=8] {'lev'}, dimensions={0} | all-to-all | bytes 409600 | tf_op jit(solution)/shard_map/all_to_all | solution.py:46
  495.6 9.1 %reduce.15 = bf16[1280,80]{1,0:T(8,128)(2,1)} reduce(bf16[1280,1,80]{2,1,0:T(2,128)(2,1)} %bitcast.311, bf16[]{:T(256)} %broadcast.798), dimensions={1}, to_apply=%bitcast.276.reduce_sub_computation | reduce | bytes 409602
  506.9 15.6 %all_to_all.203 = bf16[32,2,1600]{2,1,0:T(2,128)(2,1)} all-to-all(bf16[32,2,1600]{2,1,0:T(2,128)(2,1)} %reshape.550), channel_id=1, replica_groups=mesh['lat'=32,'lev'=8] {'lat'}, dimensions={0} | all-to-all | bytes 409600 | tf_op jit(solution)/shard_map/all_to_all | solution.py:47
  530.0 7.2 subtract_convert_fusion
  537.2 8.8 %fusion.56 = f32[80,2560]{1,0:T(8,128)S(1)} fusion(bf16[2560,2560]{0,1:T(8,128)(2,1)} %convert_element_type.137, bf16[40,2560]{1,0:T(8,128)(2,1)S(1)} %get-tuple-element.8, bf16[40,2560]{1,0:T(8,128)(2,1)S(1)} %get-tuple-element.9), kind=kOutput, calls=%fused_computation.58 | convolution fusion | flops 1049395200 | bytes 14336000 | tf_op jit(solution)/shard_map/dot_general | solution.py:95
  549.0 15.1 %reduce.16 = bf16[2560,40]{1,0:T(8,128)(2,1)} reduce(bf16[2560,1,40]{2,1,0:T(2,128)(2,1)S(1)} %bitcast.306, bf16[]{:T(256)} %broadcast.798), dimensions={1}, to_apply=%bitcast.278.reduce_sub_computation | reduce | bytes 409602
  566.2 12.5 %all_to_all.204 = bf16[32,2,1600]{2,1,0:T(2,128)(2,1)} all-to-all(bf16[32,2,1600]{2,1,0:T(2,128)(2,1)S(1)} %reshape.552), channel_id=1, replica_groups=mesh['lat'=32,'lev'=8] {'lat'}, dimensions={0} | all-to-all | bytes 409600 | tf_op jit(solution)/shard_map/all_to_all | solution.py:37
  595.5 15.1 %all_to_all.205 = bf16[8,2,6400]{2,1,0:T(2,128)(2,1)} all-to-all(bf16[8,2,6400]{2,1,0:T(2,128)(2,1)} %reshape.554), channel_id=1, replica_groups=mesh['lat'=32,'lev'=8] {'lev'}, dimensions={0} | all-to-all | bytes 409600 | tf_op jit(solution)/shard_map/all_to_all | solution.py:36
  627.7 73.1 %psum.31 = f32[]{:T(128)} all-reduce(f32[]{:T(128)} %fusion.42), channel_id=1, replica_groups=mesh['lat'=32,'lev'=8] {'lat','lev'}, use_global_device_ids=true, to_apply=%region_7.8 | all-reduce | flops 1 | bytes 8 | tf_op jit(solution)/shard_map/psum | solution.py:113
  712.9 13.3 %all-to-all-done.10 = bf16[8,1280,10]{1,2,0:T(8,128)(2,1)S(1)} async-done(((bf16[8,1280,10]{1,2,0:T(8,128)(2,1)}), bf16[8,1280,10]{1,2,0:T(8,128)(2,1)S(1)}, u32[]{:S(2)}, u32[]{:S(2)}) %all-to-all-start.10) | async-done | bytes 204832 | tf_op jit(solution)/shard_map/all_to_all | solution.py:46
  726.7 7.4 reduce.18
  740.8 7.6 all-to-all-done.11
  749.4 7.8 %convolution_bitcast_fusion = f32[1,40,2560]{2,1,0:T(8,128)} fusion(bf16[40,2560]{1,0:T(8,128)(2,1)S(1)} %reshape.534, bf16[2560,2560]{0,1:T(8,128)(2,1)} %convert_element_type.137), kind=kOutput, calls=%fused_computation.23 | convolution fusion | flops 524288000 | bytes 13721600 | tf_op jit(solution)/shard_map/dot_general | solution.py:88
  (130 shorter events, 133.9 us)
Async XLA Ops:
  93.6 27.2 %copy-start.7 = (f32[1,40,2560]{2,1,0:T(8,128)S(1)}, f32[1,40,2560]{2,1,0:T(8,128)}, u32[]{:S(2)}) copy-start(f32[1,40,2560]{2,1,0:T(8,128)} %param.6) | copy-start | bytes 1228804
  93.6 27.2 %copy-start.8 = (f32[1,40,2560]{2,1,0:T(8,128)S(1)}, f32[1,40,2560]{2,1,0:T(8,128)}, u32[]{:S(2)}) copy-start(f32[1,40,2560]{2,1,0:T(8,128)} %param.8) | copy-start | bytes 1228804
  93.6 27.2 %copy-start.9 = (s32[1,40,2560]{2,1,0:T(8,128)S(1)}, s32[1,40,2560]{2,1,0:T(8,128)}, u32[]{:S(2)}) copy-start(s32[1,40,2560]{2,1,0:T(8,128)} %param.7) | copy-start | bytes 1228804
  129.8 64.9 %copy-start.6 = (f32[8,1280]{1,0:T(8,128)S(1)}, f32[8,1280]{1,0:T(8,128)}, u32[]{:S(2)}) copy-start(f32[8,1280]{1,0:T(8,128)} %param.11) | copy-start | bytes 122884
  147.3 17.2 %all-to-all-start = ((bf16[32,2,1600]{2,1,0:T(2,128)(2,1)}), bf16[32,2,1600]{2,1,0:T(2,128)(2,1)S(1)}, u32[]{:S(2)}, u32[]{:S(2)}) async-start(bf16[32,2,1600]{2,1,0:T(2,128)(2,1)} %reshape.540), calls=%async_computation | async-start | bytes 425984 | tf_op jit(solution)/shard_map/all_to_all | solution.py:37
  170.0 18.2 %all-to-all-start.1 = ((bf16[8,2,6400]{2,1,0:T(2,128)(2,1)}), bf16[8,2,6400]{2,1,0:T(2,128)(2,1)S(1)}, u32[]{:S(2)}, u32[]{:S(2)}) async-start(bf16[8,2,6400]{2,1,0:T(2,128)(2,1)} %reshape.542), calls=%async_computation.1 | async-start | bytes 409600 | tf_op jit(solution)/shard_map/all_to_all | solution.py:36
  315.0 222.2 %copy-start = (f32[1,5,2,8,1280]{4,3,2,1,0:T(8,128)}, f32[1,5,2,8,1280]{4,3,2,1,0:T(8,128)S(1)}, u32[]{:S(2)}) copy-start(f32[1,5,2,8,1280]{4,3,2,1,0:T(8,128)S(1)} %get-tuple-element.12) | copy-start | bytes 1228804
  315.0 222.2 %copy-start.2 = (f32[1,5,2,8,1280]{4,3,2,1,0:T(8,128)}, f32[1,5,2,8,1280]{4,3,2,1,0:T(8,128)S(1)}, u32[]{:S(2)}) copy-start(f32[1,5,2,8,1280]{4,3,2,1,0:T(8,128)S(1)} %get-tuple-element.13) | copy-start | bytes 1228804
  465.0 0.7 copy-start.4
  584.4 42.4 %copy-start.1 = (f32[1,5,2,8,1280]{4,3,2,1,0:T(8,128)S(1)}, f32[1,5,2,8,1280]{4,3,2,1,0:T(8,128)}, u32[]{:S(2)}) copy-start(f32[1,5,2,8,1280]{4,3,2,1,0:T(8,128)} %copy-done) | copy-start | bytes 1228804
  584.4 42.4 %copy-start.3 = (f32[1,5,2,8,1280]{4,3,2,1,0:T(8,128)S(1)}, f32[1,5,2,8,1280]{4,3,2,1,0:T(8,128)}, u32[]{:S(2)}) copy-start(f32[1,5,2,8,1280]{4,3,2,1,0:T(8,128)} %copy-done.2) | copy-start | bytes 1228804
  584.4 117.6 %copy-start.5 = (f32[5,1,2,8,1280]{4,3,2,0,1:T(8,128)S(1)}, f32[5,1,2,8,1280]{4,3,2,0,1:T(8,128)}, u32[]{:S(2)}) copy-start(f32[5,1,2,8,1280]{4,3,2,0,1:T(8,128)} %copy-done.4) | copy-start | bytes 1228804
  709.2 16.9 %all-to-all-start.10 = ((bf16[8,1280,10]{1,2,0:T(8,128)(2,1)}), bf16[8,1280,10]{1,2,0:T(8,128)(2,1)S(1)}, u32[]{:S(2)}, u32[]{:S(2)}) async-start(bf16[8,1280,10]{1,2,0:T(8,128)(2,1)} %copy.222), calls=%async_computation.10 | async-start | bytes 655360 | tf_op jit(solution)/shard_map/all_to_all | solution.py:46
  735.5 12.9 %all-to-all-start.11 = ((bf16[32,2,1600]{2,1,0:T(2,128)(2,1)}), bf16[32,2,1600]{2,1,0:T(2,128)(2,1)S(1)}, u32[]{:S(2)}, u32[]{:S(2)}) async-start(bf16[32,2,1600]{2,1,0:T(2,128)(2,1)} %reshape.556), calls=%async_computation.11 | async-start | bytes 425984 | tf_op jit(solution)/shard_map/all_to_all | solution.py:47
where the time goes:
time: 772 us; the launch traced here: 757 us
  blocking collectives  332 us (43%)
  other arithmetic  144 us (19%)
  local copies, waits for them, and re-layouts  134 us (17%)
  matrix products  79 us (10%)
  waiting for transfers between devices  38.1 us (5%)
  starting transfers between devices  25.1 us (3%)
    psum x2, blocking collectives, squares(): return lax.psum(jnp.sum(residual * residual), ('lat', 'lev'))  147 us
    unnamed x9, other arithmetic  75.7 us
    psum x1, blocking collectives, local(): lax.psum(jnp.sum(direction * hessian_out), ('lat', 'lev'))  73.1 us
    convert_element_type x2, local copies, waits for them, and re-layouts, wave_table(): return (jnp.stack([jnp.cos(angle), jnp.sin(angle)], axis=2) * factor).res...  60.1 us
    cos x1, other arithmetic, wave_table(): jnp.cos(angle)  53.6 us
    all_to_all x2, blocking collectives, to_bands(): lax.all_to_all(sectioned, 'lat', split_axis=1, concat_axis=2, tiled=True)  31.3 us
    all_to_all x2, blocking collectives, to_owners(): lax.all_to_all(lax.all_to_all(fourier, 'lat', split_axis=2, concat_axis=1...  28.6 us
    unnamed x42, local copies, waits for them, and re-layouts  28.4 us
  transfers between devices with their start and end apart: 4, of which 4 were waited for; matrix products, arithmetic and copies ran while one was open for 0% of the time, Pallas kernels for 0%

commit v1 on v0

v1 whole, which is shorter than its diff:
```python
import functools
import math

import jax
import jax.numpy as jnp
from jax import lax
from jax.experimental import pallas as pl
from jax.experimental.pallas import tpu as pltpu
from jax.sharding import PartitionSpec as P

BF = jnp.bfloat16
F32 = jnp.float32
GROUPS = 3
SUB = 4
SPARE = 120
VMEM_LIMIT = 40 * 1024 * 1024


def iota(shape, axis):
    return lax.broadcasted_iota(jnp.int32, shape, axis)


def params():
    return pltpu.CompilerParams(vmem_limit_bytes=VMEM_LIMIT)


def mm(a, b):
    return jnp.dot(a, b, preferred_element_type=F32)


def mm_nt(a, b):
    return lax.dot_general(a, b, (((1,), (1,)), ((), ())), preferred_element_type=F32)


def pack_scalars(values):
    lane = iota((1, 128), 1)
    out = jnp.zeros((1, 128), F32)
    for index, value in enumerate(values):
        rest = jnp.zeros((1, 128), F32) + value
        for piece in range(3):
            part = rest.astype(BF).astype(F32)
            rest = rest - part
            out = jnp.where(lane == SPARE + 3 * index + piece, part, out)
    return out


def unpack_scalars(received, count):
    total = jnp.sum(received, axis=0, keepdims=True) * (1.0 / SUB)
    lane = iota((1, 128), 1)
    sums = []
    for index in range(count):
        first = SPARE + 3 * index
        sums.append(jnp.sum(jnp.where((lane >= first) & (lane < first + 3), total, 0.0)))
    return sums


def make_rhs(field, south, rows, half):
    high = field.astype(BF).astype(F32)
    low = field - high
    gap = jnp.zeros((64 - rows, half), F32)
    stacked = jnp.concatenate(
        [high[:, :half], gap, low[:, :half], gap, high[:, half:], gap, low[:, half:], gap], axis=0
    ).astype(BF)
    to = iota((256, 256), 0)
    source = iota((256, 256), 1)
    inner = to & 63
    flipped = jnp.where((south > 0) & (inner < rows), to - inner + (rows - 1) - inner, to)
    chooser = jnp.where(source == flipped, 1.0, 0.0).astype(BF)
    return mm(chooser, stacked).astype(BF)


def project(table, rhs, sign):
    product = mm_nt(table, rhs)
    both = product[:, :128] + sign * product[:, 128:]
    return both + pltpu.roll(both, 64, 1)


def column(cols, group):
    picked = cols[:, 0:1]
    for index in range(1, GROUPS):
        picked = jnp.where(group == index, cols[:, index : index + 1], picked)
    return picked


def first_kernel(rows, points, south_ref, cols_ref, inn_ref, mask_ref, weight_ref, table_ref, send_ref, rhs_ref, acc_ref):
    half = points // 2
    block = pl.program_id(0)
    group = pl.program_id(1)

    @pl.when((block == 0) & (group == 0))
    def _():
        scale = mask_ref[...].astype(F32) * weight_ref[...]
        rhs_ref[...] = make_rhs(scale * inn_ref[...], south_ref[0], rows, half)

    waves = column(cols_ref[...], group)
    count = waves.shape[0]
    place = iota((count, 1), 0) & (SUB - 1)
    valid = (group < GROUPS - 1) | (place < 2)
    factor = jnp.where(valid, math.sqrt(2.0 / points), 0.0)
    turn = (place & 1).astype(F32) * (points // 4)
    wave_f = waves.astype(F32)
    lane = iota((1, 128), 1).astype(F32)

    def cosine(raw):
        inside = raw - jnp.floor((raw + 0.5) * (1.0 / points)) * points
        angle = (jnp.abs(inside - points // 2) - points // 4) * (2.0 * math.pi / points)
        square = angle * angle
        poly = jnp.full_like(square, -1.0 / 39916800.0)
        for coefficient in (1.0 / 362880.0, -1.0 / 5040.0, 1.0 / 120.0, -1.0 / 6.0, 1.0):
            poly = poly * square + coefficient
        return poly * angle

    before = cosine(wave_f * lane - turn) * factor
    now = cosine(wave_f * (lane + 128.0) - turn) * factor
    twice = 2.0 * cosine(wave_f * 128.0)
    pieces = [before.astype(BF), now.astype(BF)]
    for _ in range(2, half // 128):
        before, now = now, twice * now - before
        pieces.append(now.astype(BF))
    for index, piece in enumerate(pieces):
        table_ref[:, 128 * index : 128 * (index + 1)] = piece
    sign = 1.0 - 2.0 * (waves & 1).astype(F32)
    placed = pltpu.roll(project(table_ref[...], rhs_ref[...], sign), group * rows, 1)
    lanes = iota((1, 128), 1)
    mine = (lanes >= group * rows) & (lanes < (group + 1) * rows)
    acc = jnp.where(mine, placed, jnp.where(group == 0, 0.0, acc_ref[...]))
    acc_ref[...] = acc

    @pl.when(group == GROUPS - 1)
    def _():
        send_ref[...] = acc.astype(BF)


def grid_synthesis(south, received, table_ref, copies, mrows, rows, points):
    half = points // 2
    source = iota((128, 128), 0)
    to = iota((128, 128), 1)
    base = jnp.where(to >= 2 * rows, 2 * rows, jnp.where(to >= rows, rows, 0))
    flipped = jnp.where((south > 0) & (to < SPARE), 2 * base + (rows - 1) - to, to)
    chooser = jnp.where((source == flipped) & (to < SPARE), 1.0, 0.0).astype(BF)
    across = mm(received, chooser).T
    signs = 1.0 - 2.0 * (mrows & 1).astype(F32)
    total = jnp.zeros((2 * rows, half), F32)
    per_group = received.shape[0]
    step = per_group * GROUPS // len(copies)
    for group in range(GROUPS):
        lines = across[rows * group : rows * (group + 1)]
        lhs = jnp.concatenate([lines, lines * signs[group : group + 1]], axis=0).astype(BF)
        for part in range(per_group // step):
            index = group * (per_group // step) + part
            copies[index].wait()
            total = total + mm(lhs[:, part * step : (part + 1) * step], table_ref[index * step : (index + 1) * step, :])
    return jnp.concatenate([total[:rows], total[rows:]], axis=1)


def start_copies(hbm_ref, vmem_ref, sems, count):
    step = hbm_ref.shape[0] // count
    copies = []
    for index in range(count):
        window = pl.ds(index * step, step)
        copies.append(pltpu.make_async_copy(hbm_ref.at[window], vmem_ref.at[window], sems.at[index]))
        copies[-1].start()
    return copies


def middle_kernel(rows, points, south_ref, x_ref, table_hbm, cols_ref, mrows_ref, mask_ref, weight_ref,
                  field_ref, send_ref, scalar_ref, table_ref, rhs_ref, sems):
    half = points // 2
    copies = start_copies(table_hbm, table_ref, sems, 6)
    received = x_ref[...]
    (norm0,) = unpack_scalars(received.astype(F32), 1)
    field = grid_synthesis(south_ref[0], received, table_ref, copies, mrows_ref[...], rows, points)
    field_ref[...] = field
    scaled = mask_ref[...].astype(F32) * weight_ref[...] * field
    energy = jnp.sum(scaled * field)
    rhs_ref[...] = make_rhs(scaled, south_ref[0], rows, half)
    scalar_ref[...] = jnp.zeros((8, 128), F32) + norm0
    extra = pack_scalars([norm0, energy])
    lanes = iota((1, 128), 1)
    per_group = x_ref.shape[0]
    step = 256

    def body(block, carry):
        start = pl.multiple_of(block * step, step)
        cols = cols_ref[pl.ds(start, step), :]
        acc = jnp.zeros((step, 128), F32) + extra
        for group in range(GROUPS):
            sign = 1.0 - 2.0 * (cols[:, group : group + 1] & 1).astype(F32)
            lines = table_ref[pl.ds(pl.multiple_of(group * per_group + block * step, step), step), :]
            placed = project(lines, rhs_ref[...], sign)
            if group > 0:
                placed = pltpu.roll(placed, group * rows, 1)
            acc = jnp.where((lanes >= group * rows) & (lanes < (group + 1) * rows), placed, acc)
        send_ref[pl.ds(start, step), :] = acc.astype(BF)
        return carry

    lax.fori_loop(0, per_group // step, body, 0)


def last_kernel(rows, points, south_ref, x_ref, table_hbm, mrows_ref, mask_ref, weight_ref, first_ref, scalar_in,
                field_ref, energy_ref, scalar_ref, table_ref, sems):
    copies = start_copies(table_hbm, table_ref, sems, 6)
    received = x_ref[...]
    norm1, cross = unpack_scalars(received.astype(F32), 2)
    norm0 = scalar_in[0:1, 0:1]
    beta = (jnp.zeros((1, 1), F32) + norm1) / norm0
    field = grid_synthesis(south_ref[0], received, table_ref, copies, mrows_ref[...], rows, points)
    field = field + beta * first_ref[...]
    field_ref[...] = field
    scaled = mask_ref[...].astype(F32) * weight_ref[...] * field
    energy_ref[...] = jnp.zeros(energy_ref.shape, F32) + jnp.sum(scaled * field)
    line = iota((8, 128), 0)
    scalar_ref[...] = jnp.where(line == 0, norm1, cross)


def lane_windows(band, rows):
    start = band * rows
    block, offset = start // 128, start % 128
    if offset + rows <= 128:
        return [(block, offset, offset + rows)]
    return [(block, offset, 128), (block + 1, 0, offset + rows - 128)]


def chooser(part, transposed):
    shape = (64, 32) if transposed else (32, 64)
    fine = iota(shape, 1 if transposed else 0)
    wide = iota(shape, 0 if transposed else 1)
    where = (fine >> 4) * 32 + (fine & 7) * SUB + 2 * part + ((fine >> 3) & 1)
    return jnp.where(wide == where, 1.0, 0.0).astype(BF)


def parity_row(wave, degrees):
    offset = iota((1, degrees), 1) - wave
    return jnp.where(offset >= 0, 1.0 - 2.0 * (offset & 1).astype(F32), 0.0)


def spectral_kernel(rows, with_base, waves_ref, x_ref, basis_hbm, spread_ref, *refs):
    if with_base:
        base_ref, out_ref, send_ref, scalar_ref, basis_ref, sems = refs
    else:
        out_ref, send_ref, scalar_ref, basis_ref, sems = refs
    owned, half_rows, degrees = basis_hbm.shape
    bands = half_rows // rows
    copies = start_copies(basis_hbm, basis_ref, sems, owned)
    received = x_ref[...].astype(F32)
    lane = iota((1, 128), 1)
    if with_base:
        norm0, energy = unpack_scalars(received, 2)
        norm0 = (jnp.zeros((1, 1), F32) + norm0) * (1.0 / (2 * bands * 8))
        step_size = norm0 / (norm0 + energy)
        scalar_ref[...] = jnp.zeros((8, 128), F32) + step_size
    spread_rows = jnp.concatenate([spread_ref[...], spread_ref[...]], axis=0)
    blocks = half_rows // 128
    lines = []
    for group in range(GROUPS):
        parts = []
        for side in range(2):
            columns = [jnp.zeros((32, 128), F32)] * blocks
            for band in range(bands):
                row = band if side == 0 else 2 * bands - 1 - band
                block = received[32 * row : 32 * row + 32]
                shift = (rows * band - rows * group) % 128
                if shift:
                    block = pltpu.roll(block, shift, 1)
                for index, low, high in lane_windows(band, rows):
                    columns[index] = jnp.where((lane >= low) & (lane < high), block, columns[index])
            parts.append(jnp.concatenate(columns, axis=1))
        lines.append(jnp.concatenate(parts, axis=0).astype(BF))
    norm = jnp.zeros((1, 1), F32)
    cross = jnp.zeros((1, 1), F32)
    parities = []
    for slot in range(owned):
        parity = parity_row(waves_ref[slot], degrees)
        parities.append(parity)
        lhs = mm(chooser(slot % 2, False), lines[slot // 2]).astype(BF)
        copies[slot].wait()
        sums = mm(lhs, basis_ref[slot])
        value = (sums[:16] * jnp.abs(parity) + parity * sums[16:]) * spread_rows
        if with_base:
            base = base_ref[slot]
            value = base - step_size * (base + value)
            cross = cross + jnp.sum(value * base)
        out_ref[slot] = value
        norm = norm + jnp.sum(value * value)
    if with_base:
        extra = pack_scalars([norm, cross])
    else:
        extra = pack_scalars([norm])
        scalar_ref[...] = jnp.zeros((8, 128), F32)
    wide = [None] * GROUPS
    for slot in range(owned):
        parity = parities[slot]
        coeff = (out_ref[slot] * spread_rows * jnp.abs(parity)).astype(BF).astype(F32)
        even = jnp.where(parity > 0, coeff, 0.0)
        odd = jnp.where(parity < 0, coeff, 0.0)
        sums = mm_nt(jnp.concatenate([even, odd], axis=0).astype(BF), basis_ref[slot])
        sides = jnp.concatenate([sums[:16] + sums[16:], sums[:16] - sums[16:]], axis=0).astype(BF)
        spreaded = mm(chooser(slot % 2, True), sides)
        group = slot // 2
        wide[group] = spreaded if wide[group] is None else wide[group] + spreaded
    for side in range(2):
        for band in range(bands):
            block = jnp.zeros((32, 128), F32) + extra
            for group in range(GROUPS):
                shift = (rows * group - rows * band) % 128
                place = rows * group
                for index, low, high in lane_windows(band, rows):
                    source = wide[group][32 * side : 32 * side + 32, 128 * index : 128 * index + 128]
                    if shift:
                        source = pltpu.roll(source, shift, 1)
                    block = jnp.where((lane >= place) & (lane < place + high - low), source, block)
                    place += high - low
            row = band if side == 0 else 2 * bands - 1 - band
            send_ref[32 * row : 32 * row + 32, :] = block.astype(BF)


SMEM = pl.BlockSpec(memory_space=pltpu.SMEM)
VMEM = pl.BlockSpec(memory_space=pltpu.VMEM)
ANY = pl.BlockSpec(memory_space=pl.ANY)


def shape(dims, dtype):
    return jax.ShapeDtypeStruct(dims, dtype)


def exchange(buffer):
    return lax.all_to_all(buffer, ("lat", "lev"), split_axis=0, concat_axis=0, tiled=True)


def local(innovation, obs_mask, obs_weight, order, basis, spread):
    lat = lax.axis_index("lat")
    lev = lax.axis_index("lev")
    devices = lax.axis_size("lat") * lax.axis_size("lev")
    owned, half_rows, degrees = basis.shape
    rows, points = innovation.shape[1:]
    half = points // 2
    chunk_rows = devices * SUB
    table_rows = GROUPS * chunk_rows
    mask = obs_mask.reshape(rows, points)
    weight = obs_weight.reshape(rows, points)
    south = (lat >= lax.axis_size("lat") // 2).astype(jnp.int32).reshape(1)
    my_waves = lax.dynamic_slice_in_dim(order, (lat * lax.axis_size("lev") + lev) * owned, owned)
    slots = jnp.pad(order.reshape(devices, owned), ((0, 0), (0, 2 * GROUPS - owned))).reshape(devices, GROUPS, 2)
    cols = jnp.repeat(slots.transpose(0, 2, 1), 2, axis=1).reshape(chunk_rows, GROUPS)
    mrows = jnp.pad(cols.T, ((0, 8 - GROUPS), (0, 0)))

    blocks = chunk_rows // 256
    table, send = pl.pallas_call(
        functools.partial(first_kernel, rows, points),
        grid=(blocks, GROUPS),
        in_specs=[
            SMEM,
            pl.BlockSpec((256, GROUPS), lambda b, g: (b, 0)),
            pl.BlockSpec((rows, points), lambda b, g: (0, 0)),
            pl.BlockSpec((rows, points), lambda b, g: (0, 0)),
            pl.BlockSpec((rows, points), lambda b, g: (0, 0)),
        ],
        out_specs=[
            pl.BlockSpec((256, half), lambda b, g: (g * blocks + b, 0)),
            pl.BlockSpec((256, 128), lambda b, g: (b, 0)),
        ],
        out_shape=[shape((table_rows, half), BF), shape((chunk_rows, 128), BF)],
        scratch_shapes=[pltpu.VMEM((256, half), BF), pltpu.VMEM((256, 128), F32)],
        compiler_params=params(),
        name="first",
    )(south, cols, innovation.reshape(rows, points), mask, weight)

    def spectral(received, base):
        with_base = base is not None
        return pl.pallas_call(
            functools.partial(spectral_kernel, rows, with_base),
            in_specs=[SMEM, VMEM, ANY, VMEM] + [VMEM] * with_base,
            out_specs=[VMEM] * 3,
            out_shape=[shape((owned, 16, degrees), F32), shape((chunk_rows, 128), BF), shape((8, 128), F32)],
            scratch_shapes=[pltpu.VMEM(basis.shape, BF), pltpu.SemaphoreType.DMA((owned,))],
            compiler_params=params(),
            name="spectral",
        )(my_waves, received, basis, spread, *([base] * with_base))

    rhs, send, _ = spectral(exchange(send), None)
    field1, send, norm0 = pl.pallas_call(
        functools.partial(middle_kernel, rows, points),
        in_specs=[SMEM, VMEM, ANY, VMEM, VMEM, VMEM, VMEM],
        out_specs=[VMEM] * 3,
        out_shape=[shape((rows, points), F32), shape((chunk_rows, 128), BF), shape((8, 128), F32)],
        scratch_shapes=[
            pltpu.VMEM((table_rows, half), BF),
            pltpu.VMEM((256, half), BF),
            pltpu.SemaphoreType.DMA((6,)),
        ],
        compiler_params=params(),
        name="middle",
    )(south, exchange(send), table, cols, mrows, mask, weight)
    residual, send, step1 = spectral(exchange(send), rhs)
    field2, energy, norms = pl.pallas_call(
        functools.partial(last_kernel, rows, points),
        in_specs=[SMEM, VMEM, ANY, VMEM, VMEM, VMEM, VMEM, VMEM],
        out_specs=[VMEM] * 3,
        out_shape=[shape((rows, points), F32), shape((devices, 128), F32), shape((8, 128), F32)],
        scratch_shapes=[pltpu.VMEM((table_rows, half), BF), pltpu.SemaphoreType.DMA((6,))],
        compiler_params=params(),
        name="last",
    )(south, exchange(send), table, mrows, mask, weight, field1, norm0)
    total = jnp.sum(exchange(energy)[:, 0])
    first = norm0[0, 0]
    norm1 = norms[0, 0]
    cross = norms[1, 0]
    beta = norm1 / first
    alpha1 = step1[0, 0]
    alpha2 = norm1 / (norm1 + 2.0 * beta * cross + beta * beta * first + total)
    control = alpha1 * rhs + alpha2 * (residual + beta * rhs)
    increment = alpha1 * field1 + alpha2 * field2
    return (control, increment.reshape(innovation.shape))


def solution(mesh):
    in_specs = (
        P("lev", "lat", None),
        P("lev", "lat", None),
        P("lev", "lat", None),
        P(),
        P(("lat", "lev"), None, None),
        P(),
    )
    out_specs = (P(("lat", "lev"), None, None), P("lev", "lat", None))
    return jax.shard_map(local, mesh=mesh, in_specs=in_specs, out_specs=out_specs, check_vma=False)
```

time: 772 us -> 183 us (0.24); the launches traced: 757 us -> 182 us
  blocking collectives: 332 us -> 42.4 us
  other arithmetic: 144 us -> 3.5 us
  local copies, waits for them, and re-layouts: 134 us -> 26 us
  matrix products: 79 us -> 0 us
  Pallas kernels: 0 us -> 38.8 us
    psum x3 -> x0, blocking collectives: 220 us -> none  [the longest x2 147 us: squares(): return lax.psum(jnp.sum(residual * residual), ('lat', 'lev'))]
    dot_general x12 -> x0, matrix products: 79 us -> none  [the longest x3 26.3 us: analysis(): product = jnp.dot(stacked, wave, preferred_element_type=jnp.float32)]
    unnamed x9 -> x0, other arithmetic: 75.7 us -> none
    all_to_all x8 -> x2, blocking collectives: 113 us -> 42.4 us  [exchange(): lax.all_to_all(buffer, ('lat', 'lev'), split_axis=0, concat_axis=0, tiled...]
    convert_element_type x5 -> x0, local copies, waits for them, and re-layouts: 60.9 us -> none  [the longest x2 60.1 us: wave_table(): return (jnp.stack([jnp.cos(angle), jnp.sin(angle)], axis=2) * factor).res...]
    cos x1 -> x0, other arithmetic: 53.6 us -> none  [wave_table(): jnp.cos(angle)]
    pallas_call x0 -> x5, Pallas kernels: none -> 38.8 us  [the longest x2 15.3 us: spectral(): pl.pallas_call(functools.partial(spectral_kernel, rows, with_base), in_sp...]
    all_to_all x30 -> x0, local copies, waits for them, and re-layouts: 26.9 us -> none  [the longest x12 12.9 us: to_owners(): lax.all_to_all(fourier, 'lat', split_axis=2, concat_axis=1, tiled=True)]
  transfers between devices with their start and end apart: 4 -> 3, of which waited for: 4 -> 3; matrix products, arithmetic and copies ran while one was open for 0% -> 1% of each run, Pallas kernels for 0% -> 0%
where the time goes in v1:
time: 183 us; the launch traced here: 182 us
  blocking collectives  42.4 us (23%)
  waiting for transfers between devices  39.3 us (21%)
  Pallas kernels  38.8 us (21%)
  starting transfers between devices  26.5 us (14%)
  local copies, waits for them, and re-layouts  26 us (14%)
  between operations  5.26 us (3%)
  other arithmetic  3.5 us (2%)
    all_to_all x2, blocking collectives, exchange(): lax.all_to_all(buffer, ('lat', 'lev'), split_axis=0, concat_axis=0, tiled...  42.4 us
    all_to_all x3, waiting for transfers between devices, exchange(): lax.all_to_all(buffer, ('lat', 'lev'), split_axis=0, concat_axis=0, tiled...  39.3 us
    all_to_all x3, starting transfers between devices, exchange(): lax.all_to_all(buffer, ('lat', 'lev'), split_axis=0, concat_axis=0, tiled...  26.5 us
    unnamed x25, local copies, waits for them, and re-layouts  20 us
    pallas_call x2, Pallas kernels, spectral(): pl.pallas_call(functools.partial(spectral_kernel, rows, with_base), in_sp...  15.3 us
    pallas_call x1, Pallas kernels, local(): pl.pallas_call(functools.partial(first_kernel, rows, points), grid=(block...  13.5 us
    pallas_call x1, Pallas kernels, local(): pl.pallas_call(functools.partial(middle_kernel, rows, points), in_specs=[...  6.45 us
  transfers between devices with their start and end apart: 3, of which 3 were waited for; matrix products, arithmetic and copies ran while one was open for 1% of the time, Pallas kernels for 0%

profile of v1, /device:TPU:1, one launch (start us, length us, event | category | flops | bytes accessed | tf_op | source)
XLA Modules:
  0.0 181.8 jit_solution(18386248715743262698)
XLA Ops:
  0.7 1.0 reshape.39
  1.9 1.1 broadcast_in_dim.3
  3.1 1.0 reshape_reshape.3
  4.3 1.0 copy-done.5
  5.3 1.0 copy-done.7
  6.3 1.0 copy-done.9
  7.3 13.5 %first.1 = (bf16[3072,1280]{1,0:T(8,128)(2,1)S(1)}, bf16[1024,128]{1,0:T(8,128)(2,1)}) custom-call(s32[1]{0:T(128)} %bitcast.south_ref, s32[1024,3]{1,0:T(8,128)S(1)} %copy.16.cols_ref, f32[40,2560]{1,0:T(8,128)S(1)} %bitcast.38, s32[40,2560]{1,0:T(8,128)S(1)} %bitcast.28, f32[40,2560]{1,0:T(8,128)S(1)} %bitcast.31), custom_call_target="tpu_custom_call" | custom-call | tf_op jit(solution)/shard_map/first/pallas_call | solution.py:348
  20.8 3.0 %copy-done.2 = bf16[3072,1280]{1,0:T(8,128)(2,1)} copy-done((bf16[3072,1280]{1,0:T(8,128)(2,1)}, bf16[3072,1280]{1,0:T(8,128)(2,1)S(1)}, u32[]{:S(2)}) %copy-start.2) | copy-done | bytes 7864344
  23.9 15.7 %all-to-all-start = ((bf16[256,4,128]{2,1,0:T(4,128)(2,1)}), bf16[256,4,128]{2,1,0:T(4,128)(2,1)S(1)}, u32[]{:S(2)}, u32[]{:S(2)}) async-start(bf16[256,4,128]{2,1,0:T(4,128)(2,1)} %bitcast.5), calls=%async_computation | async-start | bytes 524288 | tf_op jit(solution)/shard_map/all_to_all | solution.py:327
  39.5 0.8 dynamic_slice.3.waves_ref
  40.3 15.1 %all-to-all-done = bf16[256,4,128]{2,1,0:T(4,128)(2,1)S(1)} async-done(((bf16[256,4,128]{2,1,0:T(4,128)(2,1)}), bf16[256,4,128]{2,1,0:T(4,128)(2,1)S(1)}, u32[]{:S(2)}, u32[]{:S(2)}) %all-to-all-start) | async-done | bytes 262176 | tf_op jit(solution)/shard_map/all_to_all | solution.py:327
  55.4 3.3 %copy-done = bf16[5,640,1280]{2,1,0:T(8,128)(2,1)S(1)} copy-done((bf16[5,640,1280]{2,1,0:T(8,128)(2,1)S(1)}, bf16[5,640,1280]{2,1,0:T(8,128)(2,1)}, u32[]{:S(2)}) %copy-start) | copy-done | bytes 8192024
  58.7 0.8 copy-done.10
  59.5 8.0 %spectral.2 = (f32[5,16,1280]{2,1,0:T(8,128)S(1)}, bf16[1024,128]{1,0:T(8,128)(2,1)}, f32[8,128]{1,0:T(8,128)}) custom-call(s32[5]{0:T(128)S(1)} %dynamic_slice.3.waves_ref, bf16[1024,128]{1,0:T(8,128)(2,1)S(1)} %bitcast.34, bf16[5,640,1280]{2,1,0:T(8,128)(2,1)S(1)} %copy-done, f32[8,1280]{1,0:T(8,128)S(1)} %copy-done.10), custom_call_target="tpu_custom_call" | custom-call | tf_op jit(solution)/shard_map/spectral/pallas_call | solution.py:370
  67.5 5.4 %all-to-all-start.1 = ((bf16[256,4,128]{2,1,0:T(4,128)(2,1)}), bf16[256,4,128]{2,1,0:T(4,128)(2,1)S(1)}, u32[]{:S(2)}, u32[]{:S(2)}) async-start(bf16[256,4,128]{2,1,0:T(4,128)(2,1)} %bitcast.7), calls=%async_computation.1 | async-start | bytes 524288 | tf_op jit(solution)/shard_map/all_to_all | solution.py:327
  72.9 16.0 %all-to-all-done.1 = bf16[256,4,128]{2,1,0:T(4,128)(2,1)S(1)} async-done(((bf16[256,4,128]{2,1,0:T(4,128)(2,1)}), bf16[256,4,128]{2,1,0:T(4,128)(2,1)S(1)}, u32[]{:S(2)}, u32[]{:S(2)}) %all-to-all-start.1) | async-done | bytes 262176 | tf_op jit(solution)/shard_map/all_to_all | solution.py:327
  88.9 3.2 %copy-done.3 = bf16[3072,1280]{1,0:T(8,128)(2,1)S(1)} copy-done((bf16[3072,1280]{1,0:T(8,128)(2,1)S(1)}, bf16[3072,1280]{1,0:T(8,128)(2,1)}, u32[]{:S(2)}) %copy-start.3) | copy-done | bytes 7864344
  92.1 6.4 %middle.1 = (f32[40,2560]{1,0:T(8,128)S(1)}, bf16[1024,128]{1,0:T(8,128)(2,1)S(1)}, f32[8,128]{1,0:T(8,128)S(1)}) custom-call(s32[1]{0:T(128)} %bitcast.south_ref, bf16[1024,128]{1,0:T(8,128)(2,1)S(1)} %bitcast.35, bf16[3072,1280]{1,0:T(8,128)(2,1)S(1)} %copy-done.3, s32[1024,3]{1,0:T(8,128)S(1)} %copy.16.cols_ref, s32[8,1024]{1,0:T(8,128)S(1)} %pad.9.mrows_ref, ...), custom_call_target="tpu_custom_call" | custom-call | tf_op jit(solution)/shard_map/middle/pallas_call | solution.py:381
  98.6 21.3 %all_to_all.56 = bf16[256,4,128]{2,1,0:T(4,128)(2,1)S(1)} all-to-all(bf16[256,4,128]{2,1,0:T(4,128)(2,1)S(1)} %bitcast.39), channel_id=1, replica_groups=mesh['lat'=32,'lev'=8] {'lat','lev'}, dimensions={0} | all-to-all | bytes 524288 | tf_op jit(solution)/shard_map/all_to_all | solution.py:327
  119.9 3.3 %copy-done.1 = bf16[5,640,1280]{2,1,0:T(8,128)(2,1)S(1)} copy-done((bf16[5,640,1280]{2,1,0:T(8,128)(2,1)S(1)}, bf16[5,640,1280]{2,1,0:T(8,128)(2,1)}, u32[]{:S(2)}) %copy-start.1) | copy-done | bytes 8192024
  123.2 7.3 %spectral.3 = (f32[5,16,1280]{2,1,0:T(8,128)S(1)}, bf16[1024,128]{1,0:T(8,128)(2,1)S(1)}, f32[8,128]{1,0:T(8,128)S(1)}) custom-call(s32[5]{0:T(128)S(1)} %dynamic_slice.3.waves_ref, bf16[1024,128]{1,0:T(8,128)(2,1)S(1)} %bitcast.37, bf16[5,640,1280]{2,1,0:T(8,128)(2,1)S(1)} %copy-done.1, f32[8,1280]{1,0:T(8,128)S(1)} %copy-done.11, ...), custom_call_target="tpu_custom_call" | custom-call | tf_op jit(solution)/shard_map/spectral/pallas_call | solution.py:370
  130.6 21.1 %all_to_all.57 = bf16[256,4,128]{2,1,0:T(4,128)(2,1)S(1)} all-to-all(bf16[256,4,128]{2,1,0:T(4,128)(2,1)S(1)} %bitcast.40), channel_id=1, replica_groups=mesh['lat'=32,'lev'=8] {'lat','lev'}, dimensions={0} | all-to-all | bytes 524288 | tf_op jit(solution)/shard_map/all_to_all | solution.py:327
  151.7 3.2 %copy-done.4 = bf16[3072,1280]{1,0:T(8,128)(2,1)S(1)} copy-done((bf16[3072,1280]{1,0:T(8,128)(2,1)S(1)}, bf16[3072,1280]{1,0:T(8,128)(2,1)}, u32[]{:S(2)}) %copy-start.4) | copy-done | bytes 7864344
  154.9 3.5 %last.1 = (f32[40,2560]{1,0:T(8,128)S(1)}, f32[256,128]{1,0:T(8,128)}, f32[8,128]{1,0:T(8,128)S(1)}) custom-call(s32[1]{0:T(128)} %bitcast.south_ref, bf16[1024,128]{1,0:T(8,128)(2,1)S(1)} %bitcast.36, bf16[3072,1280]{1,0:T(8,128)(2,1)S(1)} %copy-done.4, s32[8,1024]{1,0:T(8,128)S(1)} %pad.9.mrows_ref, s32[40,2560]{1,0:T(8,128)S(1)} %bitcast.30, ...), custom_call_target="tpu_custom_call" | custom-call | tf_op jit(solution)/shard_map/last/pallas_call | solution.py:395
  158.5 5.4 %all-to-all-start.4 = ((f32[256,1,128]{2,1,0:T(1,128)}), f32[256,1,128]{2,1,0:T(1,128)S(1)}, u32[]{:S(2)}, u32[]{:S(2)}) async-start(f32[256,1,128]{2,1,0:T(1,128)} %bitcast.19), calls=%async_computation.4 | async-start | bytes 262144 | tf_op jit(solution)/shard_map/all_to_all | solution.py:327
  163.9 0.5 slice.17
  164.5 0.5 slice.15
  165.0 0.6 fusion
  168.8 8.3 %all-to-all-done.4 = f32[256,1,128]{2,1,0:T(1,128)S(1)} async-done(((f32[256,1,128]{2,1,0:T(1,128)}), f32[256,1,128]{2,1,0:T(1,128)S(1)}, u32[]{:S(2)}, u32[]{:S(2)}) %all-to-all-start.4) | async-done | bytes 131104 | tf_op jit(solution)/shard_map/all_to_all | solution.py:327
  177.0 0.6 slice_reduce_fusion
  178.9 1.4 multiply_add_fusion
  180.4 1.4 add_bitcast_fusion
  (21 shorter events, 0.6 us)
Async XLA Ops:
  0.6 88.3 %copy-start.8 = (f32[1,40,2560]{2,1,0:T(8,128)S(1)}, f32[1,40,2560]{2,1,0:T(8,128)}, u32[]{:S(2)}) copy-start(f32[1,40,2560]{2,1,0:T(8,128)} %param.8) | copy-start | bytes 1228804
  0.6 88.3 %copy-start.6 = (s32[1,40,2560]{2,1,0:T(8,128)S(1)}, s32[1,40,2560]{2,1,0:T(8,128)}, u32[]{:S(2)}) copy-start(s32[1,40,2560]{2,1,0:T(8,128)} %param.7) | copy-start | bytes 1228804
  4.3 1.0 copy-start.5
  5.3 1.0 copy-start.7
  6.3 1.0 copy-start.9
  20.8 3.0 %copy-start.2 = (bf16[3072,1280]{1,0:T(8,128)(2,1)}, bf16[3072,1280]{1,0:T(8,128)(2,1)S(1)}, u32[]{:S(2)}) copy-start(bf16[3072,1280]{1,0:T(8,128)(2,1)S(1)} %get-tuple-element.17.table_hbm) | copy-start | bytes 23592964
  23.9 31.5 %all-to-all-start = ((bf16[256,4,128]{2,1,0:T(4,128)(2,1)}), bf16[256,4,128]{2,1,0:T(4,128)(2,1)S(1)}, u32[]{:S(2)}, u32[]{:S(2)}) async-start(bf16[256,4,128]{2,1,0:T(4,128)(2,1)} %bitcast.5), calls=%async_computation | async-start | bytes 524288 | tf_op jit(solution)/shard_map/all_to_all | solution.py:327
  55.4 3.3 %copy-start = (bf16[5,640,1280]{2,1,0:T(8,128)(2,1)S(1)}, bf16[5,640,1280]{2,1,0:T(8,128)(2,1)}, u32[]{:S(2)}) copy-start(bf16[5,640,1280]{2,1,0:T(8,128)(2,1)} %basis_hbm.3) | copy-start | bytes 24576004
  58.7 0.8 copy-start.10
  59.5 60.4 %copy-start.11 = (f32[8,1280]{1,0:T(8,128)S(1)}, f32[8,1280]{1,0:T(8,128)}, u32[]{:S(2)}) copy-start(f32[8,1280]{1,0:T(8,128)} %spread_ref.3) | copy-start | bytes 122884
  67.5 21.4 %all-to-all-start.1 = ((bf16[256,4,128]{2,1,0:T(4,128)(2,1)}), bf16[256,4,128]{2,1,0:T(4,128)(2,1)S(1)}, u32[]{:S(2)}, u32[]{:S(2)}) async-start(bf16[256,4,128]{2,1,0:T(4,128)(2,1)} %bitcast.7), calls=%async_computation.1 | async-start | bytes 524288 | tf_op jit(solution)/shard_map/all_to_all | solution.py:327
  88.9 3.2 %copy-start.3 = (bf16[3072,1280]{1,0:T(8,128)(2,1)S(1)}, bf16[3072,1280]{1,0:T(8,128)(2,1)}, u32[]{:S(2)}) copy-start(bf16[3072,1280]{1,0:T(8,128)(2,1)} %copy-done.2) | copy-start | bytes 23592964
  119.9 3.3 %copy-start.1 = (bf16[5,640,1280]{2,1,0:T(8,128)(2,1)S(1)}, bf16[5,640,1280]{2,1,0:T(8,128)(2,1)}, u32[]{:S(2)}) copy-start(bf16[5,640,1280]{2,1,0:T(8,128)(2,1)} %basis_hbm.3) | copy-start | bytes 24576004
  151.7 3.2 %copy-start.4 = (bf16[3072,1280]{1,0:T(8,128)(2,1)S(1)}, bf16[3072,1280]{1,0:T(8,128)(2,1)}, u32[]{:S(2)}) copy-start(bf16[3072,1280]{1,0:T(8,128)(2,1)} %copy-done.2) | copy-start | bytes 23592964
  158.5 18.5 %all-to-all-start.4 = ((f32[256,1,128]{2,1,0:T(1,128)}), f32[256,1,128]{2,1,0:T(1,128)S(1)}, u32[]{:S(2)}, u32[]{:S(2)}) async-start(f32[256,1,128]{2,1,0:T(1,128)} %bitcast.19), calls=%async_computation.4 | async-start | bytes 262144 | tf_op jit(solution)/shard_map/all_to_all | solution.py:327

commit v2 on v1

v2 whole, which is shorter than its diff:
```python
import functools
import math

import jax
import jax.numpy as jnp
from jax import lax
from jax.experimental import pallas as pl
from jax.experimental.pallas import tpu as pltpu
from jax.sharding import PartitionSpec as P

BF = jnp.bfloat16
F32 = jnp.float32
GROUPS = 3
SUB = 4
SPARE = 120
VMEM_LIMIT = 20 * 1024 * 1024


def iota(shape, axis):
    return lax.broadcasted_iota(jnp.int32, shape, axis)


def params():
    return pltpu.CompilerParams(vmem_limit_bytes=VMEM_LIMIT)


def mm(a, b):
    return jnp.dot(a, b, preferred_element_type=F32)


def mm_nt(a, b):
    return lax.dot_general(a, b, (((1,), (1,)), ((), ())), preferred_element_type=F32)


def pack_scalars(values):
    lane = iota((1, 128), 1)
    out = jnp.zeros((1, 128), F32)
    for index, value in enumerate(values):
        rest = jnp.zeros((1, 128), F32) + value
        for piece in range(3):
            part = rest.astype(BF).astype(F32)
            rest = rest - part
            out = jnp.where(lane == SPARE + 3 * index + piece, part, out)
    return out


def unpack_scalars(received, count):
    total = jnp.sum(received, axis=0, keepdims=True) * (1.0 / SUB)
    lane = iota((1, 128), 1)
    sums = []
    for index in range(count):
        first = SPARE + 3 * index
        sums.append(jnp.sum(jnp.where((lane >= first) & (lane < first + 3), total, 0.0)))
    return sums


def make_rhs(field, south, rows, half):
    high = field.astype(BF).astype(F32)
    low = field - high
    gap = jnp.zeros((64 - rows, half), F32)
    stacked = jnp.concatenate(
        [high[:, :half], gap, low[:, :half], gap, high[:, half:], gap, low[:, half:], gap], axis=0
    ).astype(BF)
    to = iota((256, 256), 0)
    source = iota((256, 256), 1)
    inner = to & 63
    flipped = jnp.where((south > 0) & (inner < rows), to - inner + (rows - 1) - inner, to)
    chooser = jnp.where(source == flipped, 1.0, 0.0).astype(BF)
    return mm(chooser, stacked).astype(BF)


def project(table, rhs, sign):
    product = mm_nt(table, rhs)
    both = product[:, :128] + sign * product[:, 128:]
    return both + pltpu.roll(both, 64, 1)


def circle(steps, points):
    quarter = points // 4
    turns = jnp.floor(steps * (1.0 / quarter) + 0.5)
    angle = (steps - turns * quarter) * (2.0 * math.pi / points)
    turns = turns - 4.0 * jnp.floor(turns * 0.25)
    square = angle * angle
    sine = jnp.full_like(square, 1.0 / 362880.0)
    for coefficient in (-1.0 / 5040.0, 1.0 / 120.0, -1.0 / 6.0, 1.0):
        sine = sine * square + coefficient
    sine = sine * angle
    cosine = jnp.full_like(square, 1.0 / 40320.0)
    for coefficient in (-1.0 / 720.0, 1.0 / 24.0, -0.5, 1.0):
        cosine = cosine * square + coefficient
    swap = (turns == 1.0) | (turns == 3.0)
    first = jnp.where(swap, sine, cosine)
    second = jnp.where(swap, cosine, sine)
    first = jnp.where((turns == 1.0) | (turns == 2.0), -first, first)
    second = jnp.where(turns >= 2.0, -second, second)
    return first, second


def fill_table(cols_ref, table_ref, points):
    devices, owned = cols_ref.shape
    factor = math.sqrt(2.0 / points)
    lane = iota((1, 128), 1).astype(F32)
    size = 64

    def body(chunk, carry):
        start = pl.multiple_of(chunk * size, size)
        waves = cols_ref[pl.ds(start, size), :].astype(F32)
        jump_cos, jump_sin = circle(waves * 128.0, points)
        for slot in range(owned):
            picked = slice(slot, slot + 1)
            cos0, sin0 = circle(waves[:, picked] * lane, points)
            cos0, sin0 = cos0 * factor, sin0 * factor
            turn_cos = jump_cos[:, picked] + jnp.zeros((1, 128), F32)
            turn_sin = jump_sin[:, picked] + jnp.zeros((1, 128), F32)
            cos1 = cos0 * turn_cos - sin0 * turn_sin
            sin1 = sin0 * turn_cos + cos0 * turn_sin
            twice = 2.0 * turn_cos
            rows = [pl.ds(pl.multiple_of((2 * slot + r) * devices + start, size), size) for r in range(2)]
            for index in range(points // 256):
                window = slice(128 * index, 128 * (index + 1))
                table_ref[rows[0], window] = cos0.astype(BF)
                table_ref[rows[1], window] = sin0.astype(BF)
                cos0, cos1 = cos1, twice * cos1 - cos0
                sin0, sin1 = sin1, twice * sin1 - sin0
        return carry

    lax.fori_loop(0, devices // size, body, 0)


def in_south(owner_ref, cols_ref):
    return (owner_ref[0] >= cols_ref.shape[0] // 2).astype(jnp.int32)


def grid_analysis(field, south, extra, cols_ref, table_ref, rhs_ref, stage_ref, send_ref):
    rows, points = field.shape
    devices, owned = cols_ref.shape
    rhs_ref[...] = make_rhs(field, south, rows, points // 2)
    signs = 1.0 - 2.0 * (cols_ref[...] & 1).astype(F32)
    lanes = iota((1, 128), 1)
    for place in range(SUB):
        acc = jnp.zeros((devices, 128), F32) + extra
        for group in range(GROUPS):
            slot = 2 * group + place // 2
            if slot < owned:
                first = (2 * slot + place % 2) * devices
                lines = project(table_ref[first : first + devices, :], rhs_ref[...], signs[:, slot : slot + 1])
                if group > 0:
                    lines = pltpu.roll(lines, group * rows, 1)
                acc = jnp.where((lanes >= group * rows) & (lanes < (group + 1) * rows), lines, acc)
        stage_ref[pl.ds(place, devices, stride=SUB), :] = acc
    send_ref[...] = stage_ref[...].astype(BF)


def grid_synthesis(received, south, cols_ref, table_ref, stage_ref, rows, points):
    devices, owned = cols_ref.shape
    source = iota((128, 128), 0)
    to = iota((128, 128), 1)
    base = jnp.where(to >= 2 * rows, 2 * rows, jnp.where(to >= rows, rows, 0))
    flipped = jnp.where((south > 0) & (to < SPARE), 2 * base + (rows - 1) - to, to)
    picker = jnp.where((source == flipped) & (to < SPARE), 1.0, 0.0).astype(BF)
    stage_ref[...] = mm(received, picker)
    signs = 1.0 - 2.0 * (cols_ref[...] & 1).astype(F32)
    signs = jnp.concatenate([signs, jnp.zeros((devices, 128 - owned), F32)], axis=1).T
    total = jnp.zeros((2 * rows, points // 2), F32)
    for place in range(SUB):
        across = stage_ref[pl.ds(place, devices, stride=SUB), :].T
        for group in range(GROUPS):
            slot = 2 * group + place // 2
            if slot < owned:
                lines = across[rows * group : rows * (group + 1)]
                lhs = jnp.concatenate([lines, lines * signs[slot : slot + 1]], axis=0).astype(BF)
                first = (2 * slot + place % 2) * devices
                total = total + mm(lhs, table_ref[first : first + devices, :])
    return jnp.concatenate([total[:rows], total[rows:]], axis=1)


def first_kernel(owner_ref, cols_ref, inn_hbm, mask_hbm, weight_hbm, basis_hbm,
                 table_ref, basis_ref, scale_ref, send_ref,
                 inn_ref, mask_ref, weight_ref, rhs_ref, stage_ref, sems):
    rows, points = inn_ref.shape
    pairs = ((inn_hbm, inn_ref), (mask_hbm, mask_ref), (weight_hbm, weight_ref), (basis_hbm, basis_ref))
    copies = [pltpu.make_async_copy(a, b, sems.at[i]) for i, (a, b) in enumerate(pairs)]
    for copy in copies:
        copy.start()
    fill_table(cols_ref, table_ref, points)
    for copy in copies[:3]:
        copy.wait()
    scale = mask_ref[...].astype(F32) * weight_ref[...]
    scale_ref[...] = scale
    grid_analysis(scale * inn_ref[...], in_south(owner_ref, cols_ref), jnp.zeros((1, 128), F32),
                  cols_ref, table_ref, rhs_ref, stage_ref, send_ref)
    copies[3].wait()


def middle_kernel(owner_ref, x_ref, table_ref, cols_ref, scale_ref,
                  field_ref, send_ref, scalar_ref, rhs_ref, stage_ref):
    rows, points = scale_ref.shape
    received = x_ref[...]
    (norm0,) = unpack_scalars(received.astype(F32), 1)
    field = grid_synthesis(received, in_south(owner_ref, cols_ref), cols_ref, table_ref, stage_ref, rows, points)
    field_ref[...] = field
    scaled = scale_ref[...] * field
    energy = jnp.sum(scaled * field)
    scalar_ref[...] = jnp.zeros((8, 128), F32) + norm0
    grid_analysis(scaled, in_south(owner_ref, cols_ref), pack_scalars([norm0, energy]),
                  cols_ref, table_ref, rhs_ref, stage_ref, send_ref)


def last_kernel(owner_ref, x_ref, table_ref, cols_ref, scale_ref, first_ref, scalar_in,
                field_ref, energy_ref, scalar_ref, stage_ref):
    rows, points = scale_ref.shape
    received = x_ref[...]
    norm1, cross = unpack_scalars(received.astype(F32), 2)
    norm0 = scalar_in[0:1, 0:1]
    beta = (jnp.zeros((1, 1), F32) + norm1) / norm0
    field = grid_synthesis(received, in_south(owner_ref, cols_ref), cols_ref, table_ref, stage_ref, rows, points)
    field = field + beta * first_ref[...]
    field_ref[...] = field
    energy_ref[...] = jnp.zeros(energy_ref.shape, F32) + jnp.sum(scale_ref[...] * field * field)
    line = iota((8, 128), 0)
    scalar_ref[...] = jnp.where(line == 0, norm1, cross)


def lane_windows(band, rows):
    start = band * rows
    block, offset = start // 128, start % 128
    if offset + rows <= 128:
        return [(block, offset, offset + rows)]
    return [(block, offset, 128), (block + 1, 0, offset + rows - 128)]


def chooser(part, transposed):
    shape = (64, 32) if transposed else (32, 64)
    fine = iota(shape, 1 if transposed else 0)
    wide = iota(shape, 0 if transposed else 1)
    where = (fine >> 4) * 32 + (fine & 7) * SUB + 2 * part + ((fine >> 3) & 1)
    return jnp.where(wide == where, 1.0, 0.0).astype(BF)


def parity_row(wave, degrees):
    offset = iota((1, degrees), 1) - wave
    return jnp.where(offset >= 0, 1.0 - 2.0 * (offset & 1).astype(F32), 0.0)


def spectral_kernel(rows, with_base, owner_ref, order_ref, x_ref, basis_ref, spread_ref, *refs):
    if with_base:
        base_ref, out_ref, send_ref, scalar_ref = refs
    else:
        out_ref, send_ref, scalar_ref = refs
    owned, half_rows, degrees = basis_ref.shape
    bands = half_rows // rows
    received = x_ref[...].astype(F32)
    lane = iota((1, 128), 1)
    if with_base:
        norm0, energy = unpack_scalars(received, 2)
        norm0 = (jnp.zeros((1, 1), F32) + norm0) * (1.0 / (2 * bands * 8))
        step_size = norm0 / (norm0 + energy)
        scalar_ref[...] = jnp.zeros((8, 128), F32) + step_size
    spread_rows = jnp.concatenate([spread_ref[...], spread_ref[...]], axis=0)
    blocks = half_rows // 128
    lines = []
    for group in range(GROUPS):
        parts = []
        for side in range(2):
            columns = [jnp.zeros((32, 128), F32)] * blocks
            for band in range(bands):
                row = band if side == 0 else 2 * bands - 1 - band
                block = received[32 * row : 32 * row + 32]
                shift = (rows * band - rows * group) % 128
                if shift:
                    block = pltpu.roll(block, shift, 1)
                for index, low, high in lane_windows(band, rows):
                    columns[index] = jnp.where((lane >= low) & (lane < high), block, columns[index])
            parts.append(jnp.concatenate(columns, axis=1))
        lines.append(jnp.concatenate(parts, axis=0).astype(BF))
    norm = jnp.zeros((1, 1), F32)
    cross = jnp.zeros((1, 1), F32)
    parities = []
    for slot in range(owned):
        parity = parity_row(order_ref[owner_ref[0] * owned + slot], degrees)
        parities.append(parity)
        lhs = mm(chooser(slot % 2, False), lines[slot // 2]).astype(BF)
        sums = mm(lhs, basis_ref[slot])
        value = (sums[:16] * jnp.abs(parity) + parity * sums[16:]) * spread_rows
        if with_base:
            base = base_ref[slot]
            value = base - step_size * (base + value)
            cross = cross + jnp.sum(value * base)
        out_ref[slot] = value
        norm = norm + jnp.sum(value * value)
    if with_base:
        extra = pack_scalars([norm, cross])
    else:
        extra = pack_scalars([norm])
        scalar_ref[...] = jnp.zeros((8, 128), F32)
    wide = [None] * GROUPS
    for slot in range(owned):
        parity = parities[slot]
        coeff = (out_ref[slot] * spread_rows * jnp.abs(parity)).astype(BF).astype(F32)
        even = jnp.where(parity > 0, coeff, 0.0)
        odd = jnp.where(parity < 0, coeff, 0.0)
        sums = mm_nt(jnp.concatenate([even, odd], axis=0).astype(BF), basis_ref[slot])
        sides = jnp.concatenate([sums[:16] + sums[16:], sums[:16] - sums[16:]], axis=0).astype(BF)
        spreaded = mm(chooser(slot % 2, True), sides)
        group = slot // 2
        wide[group] = spreaded if wide[group] is None else wide[group] + spreaded
    for side in range(2):
        for band in range(bands):
            block = jnp.zeros((32, 128), F32) + extra
            for group in range(GROUPS):
                shift = (rows * group - rows * band) % 128
                place = rows * group
                for index, low, high in lane_windows(band, rows):
                    source = wide[group][32 * side : 32 * side + 32, 128 * index : 128 * index + 128]
                    if shift:
                        source = pltpu.roll(source, shift, 1)
                    block = jnp.where((lane >= place) & (lane < place + high - low), source, block)
                    place += high - low
            row = band if side == 0 else 2 * bands - 1 - band
            send_ref[32 * row : 32 * row + 32, :] = block.astype(BF)


def finish_kernel(energy_ref, norm0_ref, norms_ref, step_ref, rhs_ref, residual_ref, field1_ref, field2_ref,
                  control_ref, increment_ref):
    total = jnp.sum(energy_ref[...], axis=0, keepdims=True)[:, 0:1]
    first = norm0_ref[0:1, 0:1]
    norm1 = norms_ref[0:1, 0:1]
    cross = norms_ref[1:2, 0:1]
    step1 = step_ref[0:1, 0:1]
    beta = norm1 / first
    step2 = norm1 / (norm1 + 2.0 * beta * cross + beta * beta * first + total)
    mixed = step1 + step2 * beta
    for slot in range(rhs_ref.shape[0]):
        control_ref[slot] = mixed * rhs_ref[slot] + step2 * residual_ref[slot]
    increment_ref[...] = step1 * field1_ref[...] + step2 * field2_ref[...]


SMEM = pl.BlockSpec(memory_space=pltpu.SMEM)
VMEM = pl.BlockSpec(memory_space=pltpu.VMEM)
HBM = pl.BlockSpec(memory_space=pltpu.HBM)


def near(array):
    return pltpu.with_memory_space_constraint(array, pltpu.VMEM)


def far(array):
    return pltpu.with_memory_space_constraint(array, pltpu.HBM)


def shape(dims, dtype):
    return jax.ShapeDtypeStruct(dims, dtype)


def exchange(buffer):
    return lax.all_to_all(buffer, ("lat", "lev"), split_axis=0, concat_axis=0, tiled=True)


def local(innovation, obs_mask, obs_weight, order, basis, spread):
    lat = lax.axis_index("lat")
    lev = lax.axis_index("lev")
    devices = lax.axis_size("lat") * lax.axis_size("lev")
    owned, half_rows, degrees = basis.shape
    rows, points = innovation.shape[1:]
    half = points // 2
    chunk_rows = devices * SUB
    owner = (lat * lax.axis_size("lev") + lev).astype(jnp.int32).reshape(1)
    cols = order.reshape(devices, owned)
    table_rows = 2 * owned * devices
    stage = pltpu.VMEM((chunk_rows, 128), F32)
    rhs_part = pltpu.VMEM((256, half), BF)
    plane = (rows, points)

    table, basis, scale, send = pl.pallas_call(
        first_kernel,
        in_specs=[SMEM, VMEM, HBM, HBM, HBM, HBM],
        out_specs=[VMEM] * 4,
        out_shape=[
            pltpu.VMEM((table_rows, half), BF),
            pltpu.VMEM(basis.shape, BF),
            pltpu.VMEM(plane, F32),
            shape((chunk_rows, 128), BF),
        ],
        scratch_shapes=[pltpu.VMEM(plane, F32), pltpu.VMEM(plane, jnp.int32), pltpu.VMEM(plane, F32)]
        + [rhs_part, stage, pltpu.SemaphoreType.DMA((4,))],
        compiler_params=params(),
        name="first",
    )(owner, cols, *map(far, (innovation.reshape(plane), obs_mask.reshape(plane), obs_weight.reshape(plane), basis)))
    table, basis, scale = map(near, (table, basis, scale))

    def spectral(received, base):
        with_base = base is not None
        return pl.pallas_call(
            functools.partial(spectral_kernel, rows, with_base),
            in_specs=[SMEM, SMEM, VMEM, VMEM, VMEM] + [VMEM] * with_base,
            out_specs=[VMEM] * 3,
            out_shape=[shape((owned, 16, degrees), F32), shape((chunk_rows, 128), BF), shape((8, 128), F32)],
            compiler_params=params(),
            name="spectral",
        )(owner, order, received, basis, spread, *([base] * with_base))

    rhs, send, _ = spectral(exchange(send), None)
    field1, send, norm0 = pl.pallas_call(
        middle_kernel,
        in_specs=[SMEM, VMEM, VMEM, VMEM, VMEM],
        out_specs=[VMEM] * 3,
        out_shape=[shape(plane, F32), shape((chunk_rows, 128), BF), shape((8, 128), F32)],
        scratch_shapes=[rhs_part, stage],
        compiler_params=params(),
        name="middle",
    )(owner, exchange(send), table, cols, scale)
    residual, send, step1 = spectral(exchange(send), rhs)
    field2, energy, norms = pl.pallas_call(
        last_kernel,
        in_specs=[SMEM] + [VMEM] * 6,
        out_specs=[VMEM] * 3,
        out_shape=[shape(plane, F32), shape((devices, 128), F32), shape((8, 128), F32)],
        scratch_shapes=[stage],
        compiler_params=params(),
        name="last",
    )(owner, exchange(send), table, cols, scale, field1, norm0)
    control, increment = pl.pallas_call(
        finish_kernel,
        in_specs=[VMEM] * 8,
        out_specs=[VMEM] * 2,
        out_shape=[shape(rhs.shape, F32), shape(plane, F32)],
        compiler_params=params(),
        name="finish",
    )(exchange(energy), norm0, norms, step1, rhs, residual, field1, field2)
    return (control, increment.reshape(innovation.shape))


def solution(mesh):
    in_specs = (
        P("lev", "lat", None),
        P("lev", "lat", None),
        P("lev", "lat", None),
        P(),
        P(("lat", "lev"), None, None),
        P(),
    )
    out_specs = (P(("lat", "lev"), None, None), P("lev", "lat", None))
    return jax.shard_map(local, mesh=mesh, in_specs=in_specs, out_specs=out_specs, check_vma=False)
```

time: 183 us -> 139 us (0.76)
  blocking collectives: 42.4 us -> 113 us
  waiting for transfers between devices: 39.3 us -> 0 us
  starting transfers between devices: 26.5 us -> 0 us
  local copies, waits for them, and re-layouts: 26 us -> 0.95 us
  Pallas kernels: 38.8 us -> 23.9 us
  between operations: 5.26 us -> 0.7 us
  other arithmetic: 3.5 us -> 0 us
    all_to_all x2 -> x5, blocking collectives: 42.4 us -> 113 us  [exchange(): lax.all_to_all(buffer, ('lat', 'lev'), split_axis=0, concat_axis=0, tiled...]
    all_to_all x3 -> x0, waiting for transfers between devices: 39.3 us -> none  [exchange(): lax.all_to_all(buffer, ('lat', 'lev'), split_axis=0, concat_axis=0, tiled...]
    all_to_all x3 -> x0, starting transfers between devices: 26.5 us -> none  [exchange(): lax.all_to_all(buffer, ('lat', 'lev'), split_axis=0, concat_axis=0, tiled...]
    unnamed x25 -> x4, local copies, waits for them, and re-layouts: 20 us -> 0.01 us
    pallas_call x3 -> x4, Pallas kernels: 23.5 us -> 12.8 us  [the longest x1 5.33 us: local(): pl.pallas_call(first_kernel, in_specs=[SMEM, VMEM, HBM, HBM, HBM, HBM], o...]
    pallas_call x2, Pallas kernels: 15.3 us -> 11.1 us  [spectral(): pl.pallas_call(functools.partial(spectral_kernel, rows, with_base), in_sp...]
  transfers between devices with their start and end apart: 3 -> 0, of which waited for: 3 -> 0; matrix products, arithmetic and copies ran while one was open for 1% -> 0% of each run, Pallas kernels for 0% -> 0%
where the time goes in v2:
time: 139 us
  blocking collectives  113 us (81%)
  Pallas kernels  23.9 us (17%)
    all_to_all x5, blocking collectives, exchange(): lax.all_to_all(buffer, ('lat', 'lev'), split_axis=0, concat_axis=0, tiled...  113 us
    pallas_call x2, Pallas kernels, spectral(): pl.pallas_call(functools.partial(spectral_kernel, rows, with_base), in_sp...  11.1 us
    pallas_call x1, Pallas kernels, local(): pl.pallas_call(first_kernel, in_specs=[SMEM, VMEM, HBM, HBM, HBM, HBM], o...  5.33 us
    pallas_call x1, Pallas kernels, local(): pl.pallas_call(middle_kernel, in_specs=[SMEM, VMEM, VMEM, VMEM, VMEM], ou...  4.59 us

profile of v2, /device:TPU:1, one launch (start us, length us, event | category | flops | bytes accessed | tf_op | source)
XLA Modules:
  0.0 138.6 jit_solution(17106831343041299770)
XLA Ops:
  0.6 0.0 copy-start.1
  0.6 0.0 copy-start
  0.7 0.9 reshape.33.cols_ref
  1.6 5.3 %first.1 = (bf16[2560,1280]{1,0:T(8,128)(2,1)S(1)}, bf16[5,640,1280]{2,1,0:T(8,128)(2,1)S(1)}, f32[40,2560]{1,0:T(8,128)S(1)}, bf16[1024,128]{1,0:T(8,128)(2,1)S(1)}) custom-call(s32[1]{0:T(128)} %bitcast.owner_ref, s32[256,5]{1,0:T(8,128)S(1)} %reshape.33.cols_ref, f32[40,2560]{1,0:T(8,128)} %bitcast.27, s32[40,2560]{1,0:T(8,128)} %bitcast.28, ...), custom_call_target="tpu_custom_call" | custom-call | tf_op jit(solution)/shard_map/first/pallas_call | solution.py:374
  6.9 31.4 %all_to_all.55 = bf16[256,4,128]{2,1,0:T(4,128)(2,1)S(1)} all-to-all(bf16[256,4,128]{2,1,0:T(4,128)(2,1)S(1)} %bitcast.23), channel_id=1, replica_groups=mesh['lat'=32,'lev'=8] {'lat','lev'}, dimensions={0} | all-to-all | bytes 524288 | tf_op jit(solution)/shard_map/all_to_all | solution.py:356
  38.3 0.0 copy-done.1
  38.3 0.0 copy-done
  38.3 5.8 %spectral.2 = (f32[5,16,1280]{2,1,0:T(8,128)S(1)}, bf16[1024,128]{1,0:T(8,128)(2,1)S(1)}, f32[8,128]{1,0:T(8,128)}) custom-call(s32[1]{0:T(128)} %bitcast.owner_ref, s32[1280]{0:T(1024)S(1)} %copy-done.1, bf16[1024,128]{1,0:T(8,128)(2,1)S(1)} %bitcast.19, bf16[5,640,1280]{2,1,0:T(8,128)(2,1)S(1)} %get-tuple-element.20.basis_ref, f32[8,1280]{1,0:T(8,128)S(1)} %copy-done), custom_call_target="tpu_custom_call" | custom-call | tf_op jit(solution)/shard_map/spectral/pallas_call | solution.py:393
  44.1 21.1 %all_to_all.56 = bf16[256,4,128]{2,1,0:T(4,128)(2,1)S(1)} all-to-all(bf16[256,4,128]{2,1,0:T(4,128)(2,1)S(1)} %bitcast.24), channel_id=1, replica_groups=mesh['lat'=32,'lev'=8] {'lat','lev'}, dimensions={0} | all-to-all | bytes 524288 | tf_op jit(solution)/shard_map/all_to_all | solution.py:356
  65.2 4.6 %middle.1 = (f32[40,2560]{1,0:T(8,128)S(1)}, bf16[1024,128]{1,0:T(8,128)(2,1)S(1)}, f32[8,128]{1,0:T(8,128)S(1)}) custom-call(s32[1]{0:T(128)} %bitcast.owner_ref, bf16[1024,128]{1,0:T(8,128)(2,1)S(1)} %bitcast.20, bf16[2560,1280]{1,0:T(8,128)(2,1)S(1)} %get-tuple-element.22.table_ref, s32[256,5]{1,0:T(8,128)S(1)} %reshape.33.cols_ref, ...), custom_call_target="tpu_custom_call" | custom-call | tf_op jit(solution)/shard_map/middle/pallas_call | solution.py:403
  69.8 21.1 %all_to_all.57 = bf16[256,4,128]{2,1,0:T(4,128)(2,1)S(1)} all-to-all(bf16[256,4,128]{2,1,0:T(4,128)(2,1)S(1)} %bitcast.25), channel_id=1, replica_groups=mesh['lat'=32,'lev'=8] {'lat','lev'}, dimensions={0} | all-to-all | bytes 524288 | tf_op jit(solution)/shard_map/all_to_all | solution.py:356
  91.0 5.3 %spectral.3 = (f32[5,16,1280]{2,1,0:T(8,128)S(1)}, bf16[1024,128]{1,0:T(8,128)(2,1)S(1)}, f32[8,128]{1,0:T(8,128)S(1)}) custom-call(s32[1]{0:T(128)} %bitcast.owner_ref, s32[1280]{0:T(1024)S(1)} %copy-done.1, bf16[1024,128]{1,0:T(8,128)(2,1)S(1)} %bitcast.18, bf16[5,640,1280]{2,1,0:T(8,128)(2,1)S(1)} %get-tuple-element.20.basis_ref, f32[8,1280]{1,0:T(8,128)S(1)} %copy-done, ...), custom_call_target="tpu_custom_call" | custom-call | tf_op jit(solution)/shard_map/spectral/pallas_call | solution.py:393
  96.3 21.1 %all_to_all.58 = bf16[256,4,128]{2,1,0:T(4,128)(2,1)S(1)} all-to-all(bf16[256,4,128]{2,1,0:T(4,128)(2,1)S(1)} %bitcast.22), channel_id=1, replica_groups=mesh['lat'=32,'lev'=8] {'lat','lev'}, dimensions={0} | all-to-all | bytes 524288 | tf_op jit(solution)/shard_map/all_to_all | solution.py:356
  117.4 1.8 %last.1 = (f32[40,2560]{1,0:T(8,128)S(1)}, f32[256,128]{1,0:T(8,128)S(1)}, f32[8,128]{1,0:T(8,128)S(1)}) custom-call(s32[1]{0:T(128)} %bitcast.owner_ref, bf16[1024,128]{1,0:T(8,128)(2,1)S(1)} %bitcast.17, bf16[2560,1280]{1,0:T(8,128)(2,1)S(1)} %get-tuple-element.22.table_ref, s32[256,5]{1,0:T(8,128)S(1)} %reshape.33.cols_ref, ...), custom_call_target="tpu_custom_call" | custom-call | tf_op jit(solution)/shard_map/last/pallas_call | solution.py:413
  119.3 18.3 %all_to_all.59 = f32[256,1,128]{2,1,0:T(1,128)S(1)} all-to-all(f32[256,1,128]{2,1,0:T(1,128)S(1)} %bitcast.26), channel_id=1, replica_groups=mesh['lat'=32,'lev'=8] {'lat','lev'}, dimensions={0} | all-to-all | bytes 262144 | tf_op jit(solution)/shard_map/all_to_all | solution.py:356
  137.5 1.0 finish.1
Async XLA Ops:
  0.6 37.7 %copy-start.1 = (s32[1280]{0:T(1024)S(1)}, s32[1280]{0:T(1024)}, u32[]{:S(2)}) copy-start(s32[1280]{0:T(1024)} %order_ref.3) | copy-start | bytes 15364
  0.6 37.7 %copy-start = (f32[8,1280]{1,0:T(8,128)S(1)}, f32[8,1280]{1,0:T(8,128)}, u32[]{:S(2)}) copy-start(f32[8,1280]{1,0:T(8,128)} %spread_ref.3) | copy-start | bytes 122884

commit v3 on v2

--- a/solution.py
+++ b/solution.py
@@ -54,19 +54,45 @@
     return sums
 
 
-def make_rhs(field, south, rows, half):
-    high = field.astype(BF).astype(F32)
-    low = field - high
-    gap = jnp.zeros((64 - rows, half), F32)
+def reverse_lanes(pieces):
+    width = pieces.shape[1]
+    flip = jnp.where(iota((128, 128), 0) + iota((128, 128), 1) == 127, 1.0, 0.0).astype(BF)
+    return jnp.concatenate([mm(pieces[:, first : first + 128], flip) for first in range(width - 128, -1, -128)], axis=1)
+
+
+def split(values, count):
+    pieces = []
+    for _ in range(count):
+        pieces.append(values.astype(BF).astype(F32))
+        values = values - pieces[-1]
+    return pieces
+
+
+def make_rhs(field, south):
+    rows, points = field.shape
+    width = points // 4
+    quarters = [field[:, width * i : width * (i + 1)] for i in range(4)]
+    pieces = split(quarters[1], 2) + split(quarters[3], 2)
+    back = reverse_lanes(jnp.concatenate(pieces, axis=0).astype(BF))
+    back1 = back[:rows] + back[rows : 2 * rows]
+    back3 = back[2 * rows : 3 * rows] + back[3 * rows :]
+    gap = jnp.zeros((64 - rows, width), F32)
+
+    def bands(plain, signed):
+        parts = []
+        for piece in split(plain, 2) + split(signed, 2):
+            parts += [piece, gap]
+        return jnp.concatenate(parts, axis=0)
+
     stacked = jnp.concatenate(
-        [high[:, :half], gap, low[:, :half], gap, high[:, half:], gap, low[:, half:], gap], axis=0
+        [bands(quarters[0] + back3, quarters[2] + back1), bands(quarters[0] - back3, quarters[2] - back1)], axis=1
     ).astype(BF)
     to = iota((256, 256), 0)
     source = iota((256, 256), 1)
     inner = to & 63
     flipped = jnp.where((south > 0) & (inner < rows), to - inner + (rows - 1) - inner, to)
-    chooser = jnp.where(source == flipped, 1.0, 0.0).astype(BF)
-    return mm(chooser, stacked).astype(BF)
+    picker = jnp.where(source == flipped, 1.0, 0.0).astype(BF)
+    return mm(picker, stacked).astype(BF)
 
 
 def project(table, rhs, sign):
@@ -96,7 +122,7 @@
     return first, second
 
 
-def fill_table(cols_ref, table_ref, points):
+def fill_table(cols_ref, table_ref, turn_ref, points):
     devices, owned = cols_ref.shape
     factor = math.sqrt(2.0 / points)
     lane = iota((1, 128), 1).astype(F32)
@@ -104,11 +130,17 @@
 
     def body(chunk, carry):
         start = pl.multiple_of(chunk * size, size)
-        waves = cols_ref[pl.ds(start, size), :].astype(F32)
-        jump_cos, jump_sin = circle(waves * 128.0, points)
+        whole = cols_ref[pl.ds(start, size), :]
+        waves = whole.astype(F32)
+        half_cos, half_sin = circle(waves, 2 * points)
+        sign = 1.0 - 2.0 * (whole & 1).astype(F32)
+        gap = jnp.zeros((size, 8 - owned), F32)
+        rest = jnp.zeros((size, 128 - 24), F32)
+        turn_ref[pl.ds(start, size), :] = jnp.concatenate([half_cos, gap, half_sin, gap, sign, gap, rest], axis=1)
+        jump_cos, jump_sin = circle(waves * 256.0, 2 * points)
         for slot in range(owned):
             picked = slice(slot, slot + 1)
-            cos0, sin0 = circle(waves[:, picked] * lane, points)
+            cos0, sin0 = circle(waves[:, picked] * (2.0 * lane + 1.0), 2 * points)
             cos0, sin0 = cos0 * factor, sin0 * factor
             turn_cos = jump_cos[:, picked] + jnp.zeros((1, 128), F32)
             turn_sin = jump_sin[:, picked] + jnp.zeros((1, 128), F32)
@@ -116,7 +148,7 @@
             sin1 = sin0 * turn_cos + cos0 * turn_sin
             twice = 2.0 * turn_cos
             rows = [pl.ds(pl.multiple_of((2 * slot + r) * devices + start, size), size) for r in range(2)]
-            for index in range(points // 256):
+            for index in range(points // 512):
                 window = slice(128 * index, 128 * (index + 1))
                 table_ref[rows[0], window] = cos0.astype(BF)
                 table_ref[rows[1], window] = sin0.astype(BF)
@@ -127,93 +159,112 @@
     lax.fori_loop(0, devices // size, body, 0)
 
 
-def in_south(owner_ref, cols_ref):
-    return (owner_ref[0] >= cols_ref.shape[0] // 2).astype(jnp.int32)
-
-
-def grid_analysis(field, south, extra, cols_ref, table_ref, rhs_ref, stage_ref, send_ref):
+def in_south(owner_ref, turn_ref):
+    return (owner_ref[0] >= turn_ref.shape[0] // 2).astype(jnp.int32)
+
+
+def grid_analysis(field, south, extra, turn_ref, table_ref, rhs_ref, stage_ref, send_ref):
     rows, points = field.shape
-    devices, owned = cols_ref.shape
-    rhs_ref[...] = make_rhs(field, south, rows, points // 2)
-    signs = 1.0 - 2.0 * (cols_ref[...] & 1).astype(F32)
+    devices = turn_ref.shape[0]
+    owned = table_ref.shape[0] // (2 * devices)
+    width = points // 4
+    rhs_ref[...] = make_rhs(field, south)
+    turns = turn_ref[...]
     lanes = iota((1, 128), 1)
+    parts = [jnp.zeros((devices, 128), F32) + extra] * SUB
+    for slot in range(owned):
+        group = slot // 2
+        mine = (lanes >= group * rows) & (lanes < (group + 1) * rows)
+        sign = turns[:, 16 + slot : 17 + slot]
+        sums = []
+        for r in range(2):
+            first = (2 * slot + r) * devices
+            sums.append(project(table_ref[first : first + devices, :], rhs_ref[:, width * r : width * (r + 1)], sign))
+        half_cos = turns[:, slot : slot + 1]
+        half_sin = turns[:, 8 + slot : 9 + slot]
+        turned = [sums[0] * half_cos + sums[1] * half_sin, sums[1] * half_cos - sums[0] * half_sin]
+        for r in range(2):
+            lines = pltpu.roll(turned[r], group * rows, 1) if group > 0 else turned[r]
+            place = 2 * (slot % 2) + r
+            parts[place] = jnp.where(mine, lines, parts[place])
     for place in range(SUB):
-        acc = jnp.zeros((devices, 128), F32) + extra
-        for group in range(GROUPS):
-            slot = 2 * group + place // 2
-            if slot < owned:
-                first = (2 * slot + place % 2) * devices
-                lines = project(table_ref[first : first + devices, :], rhs_ref[...], signs[:, slot : slot + 1])
-                if group > 0:
-                    lines = pltpu.roll(lines, group * rows, 1)
-                acc = jnp.where((lanes >= group * rows) & (lanes < (group + 1) * rows), lines, acc)
-        stage_ref[pl.ds(place, devices, stride=SUB), :] = acc
+        stage_ref[pl.ds(place, devices, stride=SUB), :] = parts[place]
     send_ref[...] = stage_ref[...].astype(BF)
 
 
-def grid_synthesis(received, south, cols_ref, table_ref, stage_ref, rows, points):
-    devices, owned = cols_ref.shape
+def grid_synthesis(received, south, turn_ref, table_ref, stage_ref, rows):
+    devices = turn_ref.shape[0]
+    owned = table_ref.shape[0] // (2 * devices)
+    width = table_ref.shape[1]
     source = iota((128, 128), 0)
     to = iota((128, 128), 1)
     base = jnp.where(to >= 2 * rows, 2 * rows, jnp.where(to >= rows, rows, 0))
     flipped = jnp.where((south > 0) & (to < SPARE), 2 * base + (rows - 1) - to, to)
     picker = jnp.where((source == flipped) & (to < SPARE), 1.0, 0.0).astype(BF)
     stage_ref[...] = mm(received, picker)
-    signs = 1.0 - 2.0 * (cols_ref[...] & 1).astype(F32)
-    signs = jnp.concatenate([signs, jnp.zeros((devices, 128 - owned), F32)], axis=1).T
-    total = jnp.zeros((2 * rows, points // 2), F32)
-    for place in range(SUB):
-        across = stage_ref[pl.ds(place, devices, stride=SUB), :].T
+    turns = turn_ref[...].T
+    totals = [jnp.zeros((2 * rows, width), F32)] * 2
+    for part in range(2):
+        across = [stage_ref[pl.ds(2 * part + r, devices, stride=SUB), :].T for r in range(2)]
         for group in range(GROUPS):
-            slot = 2 * group + place // 2
+            slot = 2 * group + part
             if slot < owned:
-                lines = across[rows * group : rows * (group + 1)]
-                lhs = jnp.concatenate([lines, lines * signs[slot : slot + 1]], axis=0).astype(BF)
-                first = (2 * slot + place % 2) * devices
-                total = total + mm(lhs, table_ref[first : first + devices, :])
-    return jnp.concatenate([total[:rows], total[rows:]], axis=1)
+                cosines, sines = [lines[rows * group : rows * (group + 1)] for lines in across]
+                half_cos = turns[slot : slot + 1]
+                half_sin = turns[8 + slot : 9 + slot]
+                sign = turns[16 + slot : 17 + slot]
+                turned = [cosines * half_cos - sines * half_sin, cosines * half_sin + sines * half_cos]
+                for r in range(2):
+                    lhs = jnp.concatenate([turned[r], turned[r] * sign], axis=0).astype(BF)
+                    first = (2 * slot + r) * devices
+                    totals[r] = totals[r] + mm(lhs, table_ref[first : first + devices, :])
+    ahead = totals[0] + totals[1]
+    count = 2 * rows
+    back = reverse_lanes(jnp.concatenate(split(totals[0] - totals[1], 3), axis=0).astype(BF))
+    back = back[:count] + back[count : 2 * count] + back[2 * count :]
+    return jnp.concatenate([ahead[:rows], back[rows:], ahead[rows:], back[:rows]], axis=1)
 
 
 def first_kernel(owner_ref, cols_ref, inn_hbm, mask_hbm, weight_hbm, basis_hbm,
-                 table_ref, basis_ref, scale_ref, send_ref,
+                 table_ref, turn_ref, basis_ref, scale_ref, send_ref,
                  inn_ref, mask_ref, weight_ref, rhs_ref, stage_ref, sems):
-    rows, points = inn_ref.shape
+    points = inn_ref.shape[1]
     pairs = ((inn_hbm, inn_ref), (mask_hbm, mask_ref), (weight_hbm, weight_ref), (basis_hbm, basis_ref))
     copies = [pltpu.make_async_copy(a, b, sems.at[i]) for i, (a, b) in enumerate(pairs)]
     for copy in copies:
         copy.start()
-    fill_table(cols_ref, table_ref, points)
+    fill_table(cols_ref, table_ref, turn_ref, points)
     for copy in copies[:3]:
         copy.wait()
     scale = mask_ref[...].astype(F32) * weight_ref[...]
     scale_ref[...] = scale
-    grid_analysis(scale * inn_ref[...], in_south(owner_ref, cols_ref), jnp.zeros((1, 128), F32),
-                  cols_ref, table_ref, rhs_ref, stage_ref, send_ref)
+    grid_analysis(scale * inn_ref[...], in_south(owner_ref, turn_ref), jnp.zeros((1, 128), F32),
+                  turn_ref, table_ref, rhs_ref, stage_ref, send_ref)
     copies[3].wait()
 
 
-def middle_kernel(owner_ref, x_ref, table_ref, cols_ref, scale_ref,
+def middle_kernel(owner_ref, x_ref, table_ref, turn_ref, scale_ref,
                   field_ref, send_ref, scalar_ref, rhs_ref, stage_ref):
-    rows, points = scale_ref.shape
+    rows = scale_ref.shape[0]
+    south = in_south(owner_ref, turn_ref)
     received = x_ref[...]
     (norm0,) = unpack_scalars(received.astype(F32), 1)
-    field = grid_synthesis(received, in_south(owner_ref, cols_ref), cols_ref, table_ref, stage_ref, rows, points)
+    field = grid_synthesis(received, south, turn_ref, table_ref, stage_ref, rows)
     field_ref[...] = field
     scaled = scale_ref[...] * field
     energy = jnp.sum(scaled * field)
     scalar_ref[...] = jnp.zeros((8, 128), F32) + norm0
-    grid_analysis(scaled, in_south(owner_ref, cols_ref), pack_scalars([norm0, energy]),
-                  cols_ref, table_ref, rhs_ref, stage_ref, send_ref)
-
-
-def last_kernel(owner_ref, x_ref, table_ref, cols_ref, scale_ref, first_ref, scalar_in,
+    grid_analysis(scaled, south, pack_scalars([norm0, energy]), turn_ref, table_ref, rhs_ref, stage_ref, send_ref)
+
+
+def last_kernel(owner_ref, x_ref, table_ref, turn_ref, scale_ref, first_ref, scalar_in,
                 field_ref, energy_ref, scalar_ref, stage_ref):
-    rows, points = scale_ref.shape
+    rows = scale_ref.shape[0]
     received = x_ref[...]
     norm1, cross = unpack_scalars(received.astype(F32), 2)
     norm0 = scalar_in[0:1, 0:1]
     beta = (jnp.zeros((1, 1), F32) + norm1) / norm0
-    field = grid_synthesis(received, in_south(owner_ref, cols_ref), cols_ref, table_ref, stage_ref, rows, points)
+    field = grid_synthesis(received, in_south(owner_ref, turn_ref), turn_ref, table_ref, stage_ref, rows)
     field = field + beta * first_ref[...]
     field_ref[...] = field
     energy_ref[...] = jnp.zeros(energy_ref.shape, F32) + jnp.sum(scale_ref[...] * field * field)
@@ -246,7 +297,7 @@
     if with_base:
         base_ref, out_ref, send_ref, scalar_ref = refs
     else:
-        out_ref, send_ref, scalar_ref = refs
+        out_ref, send_ref = refs
     owned, half_rows, degrees = basis_ref.shape
     bands = half_rows // rows
     received = x_ref[...].astype(F32)
@@ -273,8 +324,8 @@
                     columns[index] = jnp.where((lane >= low) & (lane < high), block, columns[index])
             parts.append(jnp.concatenate(columns, axis=1))
         lines.append(jnp.concatenate(parts, axis=0).astype(BF))
-    norm = jnp.zeros((1, 1), F32)
-    cross = jnp.zeros((1, 1), F32)
+    norm = jnp.zeros((16, degrees), F32)
+    cross = jnp.zeros((16, degrees), F32)
     parities = []
     for slot in range(owned):
         parity = parity_row(order_ref[owner_ref[0] * owned + slot], degrees)
@@ -285,14 +336,13 @@
         if with_base:
             base = base_ref[slot]
             value = base - step_size * (base + value)
-            cross = cross + jnp.sum(value * base)
+            cross = cross + value * base
         out_ref[slot] = value
-        norm = norm + jnp.sum(value * value)
+        norm = norm + value * value
     if with_base:
-        extra = pack_scalars([norm, cross])
+        extra = pack_scalars([jnp.sum(norm), jnp.sum(cross)])
     else:
-        extra = pack_scalars([norm])
-        scalar_ref[...] = jnp.zeros((8, 128), F32)
+        extra = pack_scalars([jnp.sum(norm)])
     wide = [None] * GROUPS
     for slot in range(owned):
         parity = parities[slot]
@@ -362,21 +412,21 @@
     devices = lax.axis_size("lat") * lax.axis_size("lev")
     owned, half_rows, degrees = basis.shape
     rows, points = innovation.shape[1:]
-    half = points // 2
     chunk_rows = devices * SUB
     owner = (lat * lax.axis_size("lev") + lev).astype(jnp.int32).reshape(1)
     cols = order.reshape(devices, owned)
     table_rows = 2 * owned * devices
     stage = pltpu.VMEM((chunk_rows, 128), F32)
-    rhs_part = pltpu.VMEM((256, half), BF)
+    rhs_part = pltpu.VMEM((256, points // 2), BF)
     plane = (rows, points)
 
-    table, basis, scale, send = pl.pallas_call(
+    table, turn, basis, scale, send = pl.pallas_call(
         first_kernel,
         in_specs=[SMEM, VMEM, HBM, HBM, HBM, HBM],
-        out_specs=[VMEM] * 4,
+        out_specs=[VMEM] * 5,
         out_shape=[
-            pltpu.VMEM((table_rows, half), BF),
+            pltpu.VMEM((table_rows, points // 4), BF),
+            pltpu.VMEM((devices, 128), F32),
             pltpu.VMEM(basis.shape, BF),
             pltpu.VMEM(plane, F32),
             shape((chunk_rows, 128), BF),
@@ -386,20 +436,21 @@
         compiler_params=params(),
         name="first",
     )(owner, cols, *map(far, (innovation.reshape(plane), obs_mask.reshape(plane), obs_weight.reshape(plane), basis)))
-    table, basis, scale = map(near, (table, basis, scale))
+    table, turn, basis, scale = map(near, (table, turn, basis, scale))
 
     def spectral(received, base):
         with_base = base is not None
         return pl.pallas_call(
             functools.partial(spectral_kernel, rows, with_base),
             in_specs=[SMEM, SMEM, VMEM, VMEM, VMEM] + [VMEM] * with_base,
-            out_specs=[VMEM] * 3,
-            out_shape=[shape((owned, 16, degrees), F32), shape((chunk_rows, 128), BF), shape((8, 128), F32)],
+            out_specs=[VMEM] * (2 + with_base),
+            out_shape=[shape((owned, 16, degrees), F32), shape((chunk_rows, 128), BF)]
+            + [shape((8, 128), F32)] * with_base,
             compiler_params=params(),
             name="spectral",
         )(owner, order, received, basis, spread, *([base] * with_base))
 
-    rhs, send, _ = spectral(exchange(send), None)
+    rhs, send = spectral(exchange(send), None)
     field1, send, norm0 = pl.pallas_call(
         middle_kernel,
         in_specs=[SMEM, VMEM, VMEM, VMEM, VMEM],
@@ -408,7 +459,7 @@
         scratch_shapes=[rhs_part, stage],
         compiler_params=params(),
         name="middle",
-    )(owner, exchange(send), table, cols, scale)
+    )(owner, exchange(send), table, turn, scale)
     residual, send, step1 = spectral(exchange(send), rhs)
     field2, energy, norms = pl.pallas_call(
         last_kernel,
@@ -418,7 +469,7 @@
         scratch_shapes=[stage],
         compiler_params=params(),
         name="last",
-    )(owner, exchange(send), table, cols, scale, field1, norm0)
+    )(owner, exchange(send), table, turn, scale, field1, norm0)
     control, increment = pl.pallas_call(
         finish_kernel,
         in_specs=[VMEM] * 8,

time: 139 us -> 136 us (0.978)
  Pallas kernels: 23.9 us -> 20.7 us
where the time goes in v3:
time: 136 us
  blocking collectives  113 us (83%)
  Pallas kernels  20.7 us (15%)
    all_to_all x5, blocking collectives, exchange(): lax.all_to_all(buffer, ('lat', 'lev'), split_axis=0, concat_axis=0, tiled...  113 us
    pallas_call x2, Pallas kernels, spectral(): pl.pallas_call(functools.partial(spectral_kernel, rows, with_base), in_sp...  10.6 us
    pallas_call x1, Pallas kernels, local(): pl.pallas_call(first_kernel, in_specs=[SMEM, VMEM, HBM, HBM, HBM, HBM], o...  4.13 us
    pallas_call x1, Pallas kernels, local(): pl.pallas_call(middle_kernel, in_specs=[SMEM, VMEM, VMEM, VMEM, VMEM], ou...  3.3 us

profile of v3, /device:TPU:1, one launch (start us, length us, event | category | flops | bytes accessed | tf_op | source)
XLA Modules:
  0.0 135.6 jit_solution(10897723033970097770)
XLA Ops:
  0.6 0.0 copy-start.1
  0.6 0.0 copy-start
  0.7 0.9 reshape.33.cols_ref
  1.6 4.1 %first.1 = (bf16[2560,640]{1,0:T(8,128)(2,1)S(1)}, f32[256,128]{1,0:T(8,128)S(1)}, bf16[5,640,1280]{2,1,0:T(8,128)(2,1)S(1)}, f32[40,2560]{1,0:T(8,128)S(1)}, bf16[1024,128]{1,0:T(8,128)(2,1)S(1)}) custom-call(s32[1]{0:T(128)} %bitcast.owner_ref, s32[256,5]{1,0:T(8,128)S(1)} %reshape.33.cols_ref, f32[40,2560]{1,0:T(8,128)} %bitcast.27, s32[40,2560]{1,0:T(8,128)} %bitcast.28, ...), custom_call_target="tpu_custom_call" | custom-call | tf_op jit(solution)/shard_map/first/pallas_call | solution.py:423
  5.8 31.4 %all_to_all.55 = bf16[256,4,128]{2,1,0:T(4,128)(2,1)S(1)} all-to-all(bf16[256,4,128]{2,1,0:T(4,128)(2,1)S(1)} %bitcast.22), channel_id=1, replica_groups=mesh['lat'=32,'lev'=8] {'lat','lev'}, dimensions={0} | all-to-all | bytes 524288 | tf_op jit(solution)/shard_map/all_to_all | solution.py:406
  37.1 0.0 copy-done.1
  37.1 0.0 copy-done
  37.1 5.3 %spectral.2 = (f32[5,16,1280]{2,1,0:T(8,128)S(1)}, bf16[1024,128]{1,0:T(8,128)(2,1)S(1)}) custom-call(s32[1]{0:T(128)} %bitcast.owner_ref, s32[1280]{0:T(1024)S(1)} %copy-done.1, bf16[1024,128]{1,0:T(8,128)(2,1)S(1)} %bitcast.19, bf16[5,640,1280]{2,1,0:T(8,128)(2,1)S(1)} %get-tuple-element.21.basis_ref, f32[8,1280]{1,0:T(8,128)S(1)} %copy-done), custom_call_target="tpu_custom_call" | custom-call | tf_op jit(solution)/shard_map/spectral/pallas_call | solution.py:443
  42.4 21.1 %all_to_all.56 = bf16[256,4,128]{2,1,0:T(4,128)(2,1)S(1)} all-to-all(bf16[256,4,128]{2,1,0:T(4,128)(2,1)S(1)} %bitcast.25), channel_id=1, replica_groups=mesh['lat'=32,'lev'=8] {'lat','lev'}, dimensions={0} | all-to-all | bytes 524288 | tf_op jit(solution)/shard_map/all_to_all | solution.py:406
  63.6 3.3 %middle.1 = (f32[40,2560]{1,0:T(8,128)S(1)}, bf16[1024,128]{1,0:T(8,128)(2,1)S(1)}, f32[8,128]{1,0:T(8,128)S(1)}) custom-call(s32[1]{0:T(128)} %bitcast.owner_ref, bf16[1024,128]{1,0:T(8,128)(2,1)S(1)} %bitcast.18, bf16[2560,640]{1,0:T(8,128)(2,1)S(1)} %get-tuple-element.23.table_ref, f32[256,128]{1,0:T(8,128)S(1)} %get-tuple-element.24.turn_ref, ...), custom_call_target="tpu_custom_call" | custom-call | tf_op jit(solution)/shard_map/middle/pallas_call | solution.py:454
  66.9 21.3 %all_to_all.57 = bf16[256,4,128]{2,1,0:T(4,128)(2,1)S(1)} all-to-all(bf16[256,4,128]{2,1,0:T(4,128)(2,1)S(1)} %bitcast.24), channel_id=1, replica_groups=mesh['lat'=32,'lev'=8] {'lat','lev'}, dimensions={0} | all-to-all | bytes 524288 | tf_op jit(solution)/shard_map/all_to_all | solution.py:406
  88.2 5.3 %spectral.3 = (f32[5,16,1280]{2,1,0:T(8,128)S(1)}, bf16[1024,128]{1,0:T(8,128)(2,1)S(1)}, f32[8,128]{1,0:T(8,128)S(1)}) custom-call(s32[1]{0:T(128)} %bitcast.owner_ref, s32[1280]{0:T(1024)S(1)} %copy-done.1, bf16[1024,128]{1,0:T(8,128)(2,1)S(1)} %bitcast.17, bf16[5,640,1280]{2,1,0:T(8,128)(2,1)S(1)} %get-tuple-element.21.basis_ref, f32[8,1280]{1,0:T(8,128)S(1)} %copy-done, ...), custom_call_target="tpu_custom_call" | custom-call | tf_op jit(solution)/shard_map/spectral/pallas_call | solution.py:443
  93.5 21.1 %all_to_all.58 = bf16[256,4,128]{2,1,0:T(4,128)(2,1)S(1)} all-to-all(bf16[256,4,128]{2,1,0:T(4,128)(2,1)S(1)} %bitcast.23), channel_id=1, replica_groups=mesh['lat'=32,'lev'=8] {'lat','lev'}, dimensions={0} | all-to-all | bytes 524288 | tf_op jit(solution)/shard_map/all_to_all | solution.py:406
  114.6 1.6 %last.1 = (f32[40,2560]{1,0:T(8,128)S(1)}, f32[256,128]{1,0:T(8,128)S(1)}, f32[8,128]{1,0:T(8,128)S(1)}) custom-call(s32[1]{0:T(128)} %bitcast.owner_ref, bf16[1024,128]{1,0:T(8,128)(2,1)S(1)} %bitcast.20, bf16[2560,640]{1,0:T(8,128)(2,1)S(1)} %get-tuple-element.23.table_ref, f32[256,128]{1,0:T(8,128)S(1)} %get-tuple-element.24.turn_ref, ...), custom_call_target="tpu_custom_call" | custom-call | tf_op jit(solution)/shard_map/last/pallas_call | solution.py:464
  116.3 18.3 %all_to_all.59 = f32[256,1,128]{2,1,0:T(1,128)S(1)} all-to-all(f32[256,1,128]{2,1,0:T(1,128)S(1)} %bitcast.26), channel_id=1, replica_groups=mesh['lat'=32,'lev'=8] {'lat','lev'}, dimensions={0} | all-to-all | bytes 262144 | tf_op jit(solution)/shard_map/all_to_all | solution.py:406
  134.5 1.0 finish.1
Async XLA Ops:
  0.6 36.5 %copy-start.1 = (s32[1280]{0:T(1024)S(1)}, s32[1280]{0:T(1024)}, u32[]{:S(2)}) copy-start(s32[1280]{0:T(1024)} %order_ref.3) | copy-start | bytes 15364
  0.6 36.5 %copy-start = (f32[8,1280]{1,0:T(8,128)S(1)}, f32[8,1280]{1,0:T(8,128)}, u32[]{:S(2)}) copy-start(f32[8,1280]{1,0:T(8,128)} %spread_ref.3) | copy-start | bytes 122884

commit v4 on v3

--- a/solution.py
+++ b/solution.py
@@ -280,14 +280,6 @@
     return [(block, offset, 128), (block + 1, 0, offset + rows - 128)]
 
 
-def chooser(part, transposed):
-    shape = (64, 32) if transposed else (32, 64)
-    fine = iota(shape, 1 if transposed else 0)
-    wide = iota(shape, 0 if transposed else 1)
-    where = (fine >> 4) * 32 + (fine & 7) * SUB + 2 * part + ((fine >> 3) & 1)
-    return jnp.where(wide == where, 1.0, 0.0).astype(BF)
-
-
 def parity_row(wave, degrees):
     offset = iota((1, degrees), 1) - wave
     return jnp.where(offset >= 0, 1.0 - 2.0 * (offset & 1).astype(F32), 0.0)
@@ -295,9 +287,9 @@
 
 def spectral_kernel(rows, with_base, owner_ref, order_ref, x_ref, basis_ref, spread_ref, *refs):
     if with_base:
-        base_ref, out_ref, send_ref, scalar_ref = refs
+        base_ref, across_ref, out_ref, send_ref, scalar_ref, stage_ref = refs
     else:
-        out_ref, send_ref = refs
+        out_ref, send_ref, across_ref, stage_ref = refs
     owned, half_rows, degrees = basis_ref.shape
     bands = half_rows // rows
     received = x_ref[...].astype(F32)
@@ -308,30 +300,32 @@
         step_size = norm0 / (norm0 + energy)
         scalar_ref[...] = jnp.zeros((8, 128), F32) + step_size
     spread_rows = jnp.concatenate([spread_ref[...], spread_ref[...]], axis=0)
-    blocks = half_rows // 128
-    lines = []
-    for group in range(GROUPS):
-        parts = []
-        for side in range(2):
-            columns = [jnp.zeros((32, 128), F32)] * blocks
-            for band in range(bands):
-                row = band if side == 0 else 2 * bands - 1 - band
-                block = received[32 * row : 32 * row + 32]
-                shift = (rows * band - rows * group) % 128
-                if shift:
-                    block = pltpu.roll(block, shift, 1)
-                for index, low, high in lane_windows(band, rows):
-                    columns[index] = jnp.where((lane >= low) & (lane < high), block, columns[index])
-            parts.append(jnp.concatenate(columns, axis=1))
-        lines.append(jnp.concatenate(parts, axis=0).astype(BF))
+    stage_ref[...] = received
+    senders = [stage_ref[pl.ds(place, 2 * bands * 8, stride=SUB), :] for place in range(SUB)]
+
+    def along(place, group, side):
+        columns = [jnp.zeros((8, 128), F32)] * (half_rows // 128)
+        for band in range(bands):
+            row = band if side == 0 else 2 * bands - 1 - band
+            block = senders[place][8 * row : 8 * row + 8]
+            shift = (rows * band - rows * group) % 128
+            if shift:
+                block = pltpu.roll(block, shift, 1)
+            for index, low, high in lane_windows(band, rows):
+                columns[index] = jnp.where((lane >= low) & (lane < high), block, columns[index])
+        return jnp.concatenate(columns, axis=1)
+
     norm = jnp.zeros((16, degrees), F32)
     cross = jnp.zeros((16, degrees), F32)
     parities = []
     for slot in range(owned):
         parity = parity_row(order_ref[owner_ref[0] * owned + slot], degrees)
         parities.append(parity)
-        lhs = mm(chooser(slot % 2, False), lines[slot // 2]).astype(BF)
+        pieces = [along(2 * (slot % 2) + r, slot // 2, side) for side in range(2) for r in range(2)]
+        lhs = jnp.concatenate(pieces, axis=0).astype(BF)
         sums = mm(lhs, basis_ref[slot])
+        if not with_base:
+            across_ref[slot] = basis_ref[slot].T
         value = (sums[:16] * jnp.abs(parity) + parity * sums[16:]) * spread_rows
         if with_base:
             base = base_ref[slot]
@@ -343,31 +337,33 @@
         extra = pack_scalars([jnp.sum(norm), jnp.sum(cross)])
     else:
         extra = pack_scalars([jnp.sum(norm)])
-    wide = [None] * GROUPS
+    sides = []
     for slot in range(owned):
         parity = parities[slot]
         coeff = (out_ref[slot] * spread_rows * jnp.abs(parity)).astype(BF).astype(F32)
         even = jnp.where(parity > 0, coeff, 0.0)
         odd = jnp.where(parity < 0, coeff, 0.0)
-        sums = mm_nt(jnp.concatenate([even, odd], axis=0).astype(BF), basis_ref[slot])
-        sides = jnp.concatenate([sums[:16] + sums[16:], sums[:16] - sums[16:]], axis=0).astype(BF)
-        spreaded = mm(chooser(slot % 2, True), sides)
-        group = slot // 2
-        wide[group] = spreaded if wide[group] is None else wide[group] + spreaded
+        sums = mm(jnp.concatenate([even, odd], axis=0).astype(BF), across_ref[slot])
+        sides.append((sums[:16] + sums[16:], sums[:16] - sums[16:]))
     for side in range(2):
         for band in range(bands):
-            block = jnp.zeros((32, 128), F32) + extra
-            for group in range(GROUPS):
-                shift = (rows * group - rows * band) % 128
-                place = rows * group
-                for index, low, high in lane_windows(band, rows):
-                    source = wide[group][32 * side : 32 * side + 32, 128 * index : 128 * index + 128]
-                    if shift:
-                        source = pltpu.roll(source, shift, 1)
-                    block = jnp.where((lane >= place) & (lane < place + high - low), source, block)
-                    place += high - low
             row = band if side == 0 else 2 * bands - 1 - band
-            send_ref[32 * row : 32 * row + 32, :] = block.astype(BF)
+            for place in range(SUB):
+                block = jnp.zeros((8, 128), F32) + extra
+                for group in range(GROUPS):
+                    slot = 2 * group + place // 2
+                    if slot < owned:
+                        lines = sides[slot][side][8 * (place % 2) : 8 * (place % 2) + 8]
+                        shift = (rows * group - rows * band) % 128
+                        start = rows * group
+                        for index, low, high in lane_windows(band, rows):
+                            source = lines[:, 128 * index : 128 * index + 128]
+                            if shift:
+                                source = pltpu.roll(source, shift, 1)
+                            block = jnp.where((lane >= start) & (lane < start + high - low), source, block)
+                            start += high - low
+                stage_ref[pl.ds(32 * row + place, 8, stride=SUB), :] = block
+    send_ref[...] = stage_ref[...].astype(BF)
 
 
 def finish_kernel(energy_ref, norm0_ref, norms_ref, step_ref, rhs_ref, residual_ref, field1_ref, field2_ref,
@@ -438,19 +434,21 @@
     )(owner, cols, *map(far, (innovation.reshape(plane), obs_mask.reshape(plane), obs_weight.reshape(plane), basis)))
     table, turn, basis, scale = map(near, (table, turn, basis, scale))
 
-    def spectral(received, base):
-        with_base = base is not None
+    def spectral(received, *more):
+        with_base = len(more) > 0
         return pl.pallas_call(
             functools.partial(spectral_kernel, rows, with_base),
-            in_specs=[SMEM, SMEM, VMEM, VMEM, VMEM] + [VMEM] * with_base,
-            out_specs=[VMEM] * (2 + with_base),
+            in_specs=[SMEM, SMEM, VMEM, VMEM, VMEM] + [VMEM] * len(more),
+            out_specs=[VMEM] * 3,
             out_shape=[shape((owned, 16, degrees), F32), shape((chunk_rows, 128), BF)]
-            + [shape((8, 128), F32)] * with_base,
+            + [shape((8, 128), F32) if with_base else pltpu.VMEM((owned, degrees, half_rows), BF)],
+            scratch_shapes=[stage],
             compiler_params=params(),
             name="spectral",
-        )(owner, order, received, basis, spread, *([base] * with_base))
-
-    rhs, send = spectral(exchange(send), None)
+        )(owner, order, received, basis, spread, *more)
+
+    rhs, send, across = spectral(exchange(send))
+    across = near(across)
     field1, send, norm0 = pl.pallas_call(
         middle_kernel,
         in_specs=[SMEM, VMEM, VMEM, VMEM, VMEM],
@@ -460,7 +458,7 @@
         compiler_params=params(),
         name="middle",
     )(owner, exchange(send), table, turn, scale)
-    residual, send, step1 = spectral(exchange(send), rhs)
+    residual, send, step1 = spectral(exchange(send), rhs, across)
     field2, energy, norms = pl.pallas_call(
         last_kernel,
         in_specs=[SMEM] + [VMEM] * 6,

time: 136 us -> 133 us (0.978)
  Pallas kernels: 20.7 us -> 18.1 us
    pallas_call x2, Pallas kernels: 10.6 us -> 8.02 us  [spectral(): pl.pallas_call(functools.partial(spectral_kernel, rows, with_base), in_sp...]
where the time goes in v4:
time: 133 us
  blocking collectives  113 us (85%)
  Pallas kernels  18.1 us (14%)
    all_to_all x5, blocking collectives, exchange(): lax.all_to_all(buffer, ('lat', 'lev'), split_axis=0, concat_axis=0, tiled...  113 us
    pallas_call x2, Pallas kernels, spectral(): pl.pallas_call(functools.partial(spectral_kernel, rows, with_base), in_sp...  8.02 us
    pallas_call x1, Pallas kernels, local(): pl.pallas_call(first_kernel, in_specs=[SMEM, VMEM, HBM, HBM, HBM, HBM], o...  4.13 us
    pallas_call x1, Pallas kernels, local(): pl.pallas_call(middle_kernel, in_specs=[SMEM, VMEM, VMEM, VMEM, VMEM], ou...  3.28 us

profile of v4, /device:TPU:1, one launch (start us, length us, event | category | flops | bytes accessed | tf_op | source)
XLA Modules:
  0.0 132.9 jit_solution(13116117100648600952)
XLA Ops:
  0.6 0.0 copy-start.1
  0.6 0.0 copy-start
  0.7 0.9 reshape.33.cols_ref
  1.6 4.1 %first.1 = (bf16[2560,640]{1,0:T(8,128)(2,1)S(1)}, f32[256,128]{1,0:T(8,128)S(1)}, bf16[5,640,1280]{2,1,0:T(8,128)(2,1)S(1)}, f32[40,2560]{1,0:T(8,128)S(1)}, bf16[1024,128]{1,0:T(8,128)(2,1)S(1)}) custom-call(s32[1]{0:T(128)} %bitcast.owner_ref, s32[256,5]{1,0:T(8,128)S(1)} %reshape.33.cols_ref, f32[40,2560]{1,0:T(8,128)} %bitcast.27, s32[40,2560]{1,0:T(8,128)} %bitcast.28, ...), custom_call_target="tpu_custom_call" | custom-call | tf_op jit(solution)/shard_map/first/pallas_call | solution.py:419
  5.7 31.4 %all_to_all.55 = bf16[256,4,128]{2,1,0:T(4,128)(2,1)S(1)} all-to-all(bf16[256,4,128]{2,1,0:T(4,128)(2,1)S(1)} %bitcast.22), channel_id=1, replica_groups=mesh['lat'=32,'lev'=8] {'lat','lev'}, dimensions={0} | all-to-all | bytes 524288 | tf_op jit(solution)/shard_map/all_to_all | solution.py:402
  37.1 0.0 copy-done.1
  37.1 0.0 copy-done
  37.1 4.4 %spectral.2 = (f32[5,16,1280]{2,1,0:T(8,128)S(1)}, bf16[1024,128]{1,0:T(8,128)(2,1)S(1)}, bf16[5,1280,640]{2,1,0:T(8,128)(2,1)S(1)}) custom-call(s32[1]{0:T(128)} %bitcast.owner_ref, s32[1280]{0:T(1024)S(1)} %copy-done.1, bf16[1024,128]{1,0:T(8,128)(2,1)S(1)} %bitcast.19, bf16[5,640,1280]{2,1,0:T(8,128)(2,1)S(1)} %get-tuple-element.22.basis_ref, ...), custom_call_target="tpu_custom_call" | custom-call | tf_op jit(solution)/shard_map/spectral/pallas_call | solution.py:439
  41.5 21.1 %all_to_all.56 = bf16[256,4,128]{2,1,0:T(4,128)(2,1)S(1)} all-to-all(bf16[256,4,128]{2,1,0:T(4,128)(2,1)S(1)} %bitcast.24), channel_id=1, replica_groups=mesh['lat'=32,'lev'=8] {'lat','lev'}, dimensions={0} | all-to-all | bytes 524288 | tf_op jit(solution)/shard_map/all_to_all | solution.py:402
  62.6 3.3 %middle.1 = (f32[40,2560]{1,0:T(8,128)S(1)}, bf16[1024,128]{1,0:T(8,128)(2,1)S(1)}, f32[8,128]{1,0:T(8,128)S(1)}) custom-call(s32[1]{0:T(128)} %bitcast.owner_ref, bf16[1024,128]{1,0:T(8,128)(2,1)S(1)} %bitcast.18, bf16[2560,640]{1,0:T(8,128)(2,1)S(1)} %get-tuple-element.24.table_ref, f32[256,128]{1,0:T(8,128)S(1)} %get-tuple-element.25.turn_ref, ...), custom_call_target="tpu_custom_call" | custom-call | tf_op jit(solution)/shard_map/middle/pallas_call | solution.py:452
  65.9 21.3 %all_to_all.57 = bf16[256,4,128]{2,1,0:T(4,128)(2,1)S(1)} all-to-all(bf16[256,4,128]{2,1,0:T(4,128)(2,1)S(1)} %bitcast.25), channel_id=1, replica_groups=mesh['lat'=32,'lev'=8] {'lat','lev'}, dimensions={0} | all-to-all | bytes 524288 | tf_op jit(solution)/shard_map/all_to_all | solution.py:402
  87.2 3.6 %spectral.3 = (f32[5,16,1280]{2,1,0:T(8,128)S(1)}, bf16[1024,128]{1,0:T(8,128)(2,1)S(1)}, f32[8,128]{1,0:T(8,128)S(1)}) custom-call(s32[1]{0:T(128)} %bitcast.owner_ref, s32[1280]{0:T(1024)S(1)} %copy-done.1, bf16[1024,128]{1,0:T(8,128)(2,1)S(1)} %bitcast.17, bf16[5,640,1280]{2,1,0:T(8,128)(2,1)S(1)} %get-tuple-element.22.basis_ref, f32[8,1280]{1,0:T(8,128)S(1)} %copy-done, ...), custom_call_target="tpu_custom_call" | custom-call | tf_op jit(solution)/shard_map/spectral/pallas_call | solution.py:439
  90.8 21.1 %all_to_all.58 = bf16[256,4,128]{2,1,0:T(4,128)(2,1)S(1)} all-to-all(bf16[256,4,128]{2,1,0:T(4,128)(2,1)S(1)} %bitcast.23), channel_id=1, replica_groups=mesh['lat'=32,'lev'=8] {'lat','lev'}, dimensions={0} | all-to-all | bytes 524288 | tf_op jit(solution)/shard_map/all_to_all | solution.py:402
  112.0 1.6 %last.1 = (f32[40,2560]{1,0:T(8,128)S(1)}, f32[256,128]{1,0:T(8,128)S(1)}, f32[8,128]{1,0:T(8,128)S(1)}) custom-call(s32[1]{0:T(128)} %bitcast.owner_ref, bf16[1024,128]{1,0:T(8,128)(2,1)S(1)} %bitcast.20, bf16[2560,640]{1,0:T(8,128)(2,1)S(1)} %get-tuple-element.24.table_ref, f32[256,128]{1,0:T(8,128)S(1)} %get-tuple-element.25.turn_ref, ...), custom_call_target="tpu_custom_call" | custom-call | tf_op jit(solution)/shard_map/last/pallas_call | solution.py:462
  113.6 18.3 %all_to_all.59 = f32[256,1,128]{2,1,0:T(1,128)S(1)} all-to-all(f32[256,1,128]{2,1,0:T(1,128)S(1)} %bitcast.26), channel_id=1, replica_groups=mesh['lat'=32,'lev'=8] {'lat','lev'}, dimensions={0} | all-to-all | bytes 262144 | tf_op jit(solution)/shard_map/all_to_all | solution.py:402
  131.9 1.0 finish.1
Async XLA Ops:
  0.6 36.5 %copy-start.1 = (s32[1280]{0:T(1024)S(1)}, s32[1280]{0:T(1024)}, u32[]{:S(2)}) copy-start(s32[1280]{0:T(1024)} %order_ref.3) | copy-start | bytes 15364
  0.6 36.5 %copy-start = (f32[8,1280]{1,0:T(8,128)S(1)}, f32[8,1280]{1,0:T(8,128)}, u32[]{:S(2)}) copy-start(f32[8,1280]{1,0:T(8,128)} %spread_ref.3) | copy-start | bytes 122884

commit v5 on v4

--- a/solution.py
+++ b/solution.py
@@ -102,10 +102,8 @@
 
 
 def circle(steps, points):
-    quarter = points // 4
-    turns = jnp.floor(steps * (1.0 / quarter) + 0.5)
-    angle = (steps - turns * quarter) * (2.0 * math.pi / points)
-    turns = turns - 4.0 * jnp.floor(turns * 0.25)
+    turns = jnp.floor(steps * (1.0 / points) + 0.5)
+    angle = (steps - turns * points) * (0.5 * math.pi / points)
     square = angle * angle
     sine = jnp.full_like(square, 1.0 / 362880.0)
     for coefficient in (-1.0 / 5040.0, 1.0 / 120.0, -1.0 / 6.0, 1.0):
@@ -114,12 +112,10 @@
     cosine = jnp.full_like(square, 1.0 / 40320.0)
     for coefficient in (-1.0 / 720.0, 1.0 / 24.0, -0.5, 1.0):
         cosine = cosine * square + coefficient
-    swap = (turns == 1.0) | (turns == 3.0)
-    first = jnp.where(swap, sine, cosine)
-    second = jnp.where(swap, cosine, sine)
-    first = jnp.where((turns == 1.0) | (turns == 2.0), -first, first)
-    second = jnp.where(turns >= 2.0, -second, second)
-    return first, second
+    for _ in range(2):
+        twice = sine + sine
+        cosine, sine = 1.0 - twice * sine, twice * cosine
+    return cosine, sine
 
 
 def fill_table(cols_ref, table_ref, turn_ref, points):
@@ -337,32 +333,30 @@
         extra = pack_scalars([jnp.sum(norm), jnp.sum(cross)])
     else:
         extra = pack_scalars([jnp.sum(norm)])
-    sides = []
     for slot in range(owned):
         parity = parities[slot]
         coeff = (out_ref[slot] * spread_rows * jnp.abs(parity)).astype(BF).astype(F32)
         even = jnp.where(parity > 0, coeff, 0.0)
         odd = jnp.where(parity < 0, coeff, 0.0)
         sums = mm(jnp.concatenate([even, odd], axis=0).astype(BF), across_ref[slot])
-        sides.append((sums[:16] + sums[16:], sums[:16] - sums[16:]))
-    for side in range(2):
-        for band in range(bands):
-            row = band if side == 0 else 2 * bands - 1 - band
-            for place in range(SUB):
-                block = jnp.zeros((8, 128), F32) + extra
-                for group in range(GROUPS):
-                    slot = 2 * group + place // 2
-                    if slot < owned:
-                        lines = sides[slot][side][8 * (place % 2) : 8 * (place % 2) + 8]
-                        shift = (rows * group - rows * band) % 128
-                        start = rows * group
-                        for index, low, high in lane_windows(band, rows):
-                            source = lines[:, 128 * index : 128 * index + 128]
-                            if shift:
-                                source = pltpu.roll(source, shift, 1)
-                            block = jnp.where((lane >= start) & (lane < start + high - low), source, block)
-                            start += high - low
-                stage_ref[pl.ds(32 * row + place, 8, stride=SUB), :] = block
+        sides = (sums[:16] + sums[16:], sums[:16] - sums[16:])
+        group = slot // 2
+        for side in range(2):
+            for band in range(bands):
+                row = band if side == 0 else 2 * bands - 1 - band
+                for r in range(2):
+                    lines = sides[side][8 * r : 8 * r + 8]
+                    window = pl.ds(32 * row + 2 * (slot % 2) + r, 8, stride=SUB)
+                    block = stage_ref[window, :] if group > 0 else jnp.zeros((8, 128), F32) + extra
+                    shift = (rows * group - rows * band) % 128
+                    start = rows * group
+                    for index, low, high in lane_windows(band, rows):
+                        source = lines[:, 128 * index : 128 * index + 128]
+                        if shift:
+                            source = pltpu.roll(source, shift, 1)
+                        block = jnp.where((lane >= start) & (lane < start + high - low), source, block)
+                        start += high - low
+                    stage_ref[window, :] = block
     send_ref[...] = stage_ref[...].astype(BF)
 
 

time: 133 us -> 133 us (level)
  no operation moved by 1% of the time
where the time goes in v5:
time: 133 us; the launch traced here: 132 us
  blocking collectives  113 us (85%)
  Pallas kernels  17.6 us (13%)
    all_to_all x5, blocking collectives, exchange(): lax.all_to_all(buffer, ('lat', 'lev'), split_axis=0, concat_axis=0, tiled...  113 us
    pallas_call x2, Pallas kernels, spectral(): pl.pallas_call(functools.partial(spectral_kernel, rows, with_base), in_sp...  7.7 us
    pallas_call x1, Pallas kernels, local(): pl.pallas_call(first_kernel, in_specs=[SMEM, VMEM, HBM, HBM, HBM, HBM], o...  3.97 us
    pallas_call x1, Pallas kernels, local(): pl.pallas_call(middle_kernel, in_specs=[SMEM, VMEM, VMEM, VMEM, VMEM], ou...  3.26 us

profile of v5, /device:TPU:1, one launch (start us, length us, event | category | flops | bytes accessed | tf_op | source)
XLA Modules:
  0.0 132.5 jit_solution(12769600083370199953)
XLA Ops:
  0.6 0.0 copy-start.1
  0.6 0.0 copy-start
  0.7 0.9 reshape.33.cols_ref
  1.6 4.0 %first.1 = (bf16[2560,640]{1,0:T(8,128)(2,1)S(1)}, f32[256,128]{1,0:T(8,128)S(1)}, bf16[5,640,1280]{2,1,0:T(8,128)(2,1)S(1)}, f32[40,2560]{1,0:T(8,128)S(1)}, bf16[1024,128]{1,0:T(8,128)(2,1)S(1)}) custom-call(s32[1]{0:T(128)} %bitcast.owner_ref, s32[256,5]{1,0:T(8,128)S(1)} %reshape.33.cols_ref, f32[40,2560]{1,0:T(8,128)} %bitcast.27, s32[40,2560]{1,0:T(8,128)} %bitcast.28, ...), custom_call_target="tpu_custom_call" | custom-call | tf_op jit(solution)/shard_map/first/pallas_call | solution.py:413
  5.6 31.4 %all_to_all.55 = bf16[256,4,128]{2,1,0:T(4,128)(2,1)S(1)} all-to-all(bf16[256,4,128]{2,1,0:T(4,128)(2,1)S(1)} %bitcast.22), channel_id=1, replica_groups=mesh['lat'=32,'lev'=8] {'lat','lev'}, dimensions={0} | all-to-all | bytes 524288 | tf_op jit(solution)/shard_map/all_to_all | solution.py:396
  36.9 0.0 copy-done.1
  37.0 0.0 copy-done
  37.0 4.1 %spectral.2 = (f32[5,16,1280]{2,1,0:T(8,128)S(1)}, bf16[1024,128]{1,0:T(8,128)(2,1)S(1)}, bf16[5,1280,640]{2,1,0:T(8,128)(2,1)S(1)}) custom-call(s32[1]{0:T(128)} %bitcast.owner_ref, s32[1280]{0:T(1024)S(1)} %copy-done.1, bf16[1024,128]{1,0:T(8,128)(2,1)S(1)} %bitcast.19, bf16[5,640,1280]{2,1,0:T(8,128)(2,1)S(1)} %get-tuple-element.22.basis_ref, ...), custom_call_target="tpu_custom_call" | custom-call | tf_op jit(solution)/shard_map/spectral/pallas_call | solution.py:433
  41.0 21.1 %all_to_all.56 = bf16[256,4,128]{2,1,0:T(4,128)(2,1)S(1)} all-to-all(bf16[256,4,128]{2,1,0:T(4,128)(2,1)S(1)} %bitcast.24), channel_id=1, replica_groups=mesh['lat'=32,'lev'=8] {'lat','lev'}, dimensions={0} | all-to-all | bytes 524288 | tf_op jit(solution)/shard_map/all_to_all | solution.py:396
  62.2 3.3 %middle.1 = (f32[40,2560]{1,0:T(8,128)S(1)}, bf16[1024,128]{1,0:T(8,128)(2,1)S(1)}, f32[8,128]{1,0:T(8,128)S(1)}) custom-call(s32[1]{0:T(128)} %bitcast.owner_ref, bf16[1024,128]{1,0:T(8,128)(2,1)S(1)} %bitcast.18, bf16[2560,640]{1,0:T(8,128)(2,1)S(1)} %get-tuple-element.24.table_ref, f32[256,128]{1,0:T(8,128)S(1)} %get-tuple-element.25.turn_ref, ...), custom_call_target="tpu_custom_call" | custom-call | tf_op jit(solution)/shard_map/middle/pallas_call | solution.py:446
  65.4 21.3 %all_to_all.57 = bf16[256,4,128]{2,1,0:T(4,128)(2,1)S(1)} all-to-all(bf16[256,4,128]{2,1,0:T(4,128)(2,1)S(1)} %bitcast.25), channel_id=1, replica_groups=mesh['lat'=32,'lev'=8] {'lat','lev'}, dimensions={0} | all-to-all | bytes 524288 | tf_op jit(solution)/shard_map/all_to_all | solution.py:396
  86.7 3.6 %spectral.3 = (f32[5,16,1280]{2,1,0:T(8,128)S(1)}, bf16[1024,128]{1,0:T(8,128)(2,1)S(1)}, f32[8,128]{1,0:T(8,128)S(1)}) custom-call(s32[1]{0:T(128)} %bitcast.owner_ref, s32[1280]{0:T(1024)S(1)} %copy-done.1, bf16[1024,128]{1,0:T(8,128)(2,1)S(1)} %bitcast.17, bf16[5,640,1280]{2,1,0:T(8,128)(2,1)S(1)} %get-tuple-element.22.basis_ref, f32[8,1280]{1,0:T(8,128)S(1)} %copy-done, ...), custom_call_target="tpu_custom_call" | custom-call | tf_op jit(solution)/shard_map/spectral/pallas_call | solution.py:433
  90.4 21.1 %all_to_all.58 = bf16[256,4,128]{2,1,0:T(4,128)(2,1)S(1)} all-to-all(bf16[256,4,128]{2,1,0:T(4,128)(2,1)S(1)} %bitcast.23), channel_id=1, replica_groups=mesh['lat'=32,'lev'=8] {'lat','lev'}, dimensions={0} | all-to-all | bytes 524288 | tf_op jit(solution)/shard_map/all_to_all | solution.py:396
  111.5 1.6 %last.1 = (f32[40,2560]{1,0:T(8,128)S(1)}, f32[256,128]{1,0:T(8,128)S(1)}, f32[8,128]{1,0:T(8,128)S(1)}) custom-call(s32[1]{0:T(128)} %bitcast.owner_ref, bf16[1024,128]{1,0:T(8,128)(2,1)S(1)} %bitcast.20, bf16[2560,640]{1,0:T(8,128)(2,1)S(1)} %get-tuple-element.24.table_ref, f32[256,128]{1,0:T(8,128)S(1)} %get-tuple-element.25.turn_ref, ...), custom_call_target="tpu_custom_call" | custom-call | tf_op jit(solution)/shard_map/last/pallas_call | solution.py:456
  113.1 18.3 %all_to_all.59 = f32[256,1,128]{2,1,0:T(1,128)S(1)} all-to-all(f32[256,1,128]{2,1,0:T(1,128)S(1)} %bitcast.26), channel_id=1, replica_groups=mesh['lat'=32,'lev'=8] {'lat','lev'}, dimensions={0} | all-to-all | bytes 262144 | tf_op jit(solution)/shard_map/all_to_all | solution.py:396
  131.4 1.0 finish.1
Async XLA Ops:
  0.6 36.3 %copy-start.1 = (s32[1280]{0:T(1024)S(1)}, s32[1280]{0:T(1024)}, u32[]{:S(2)}) copy-start(s32[1280]{0:T(1024)} %order_ref.3) | copy-start | bytes 15364
  0.6 36.3 %copy-start = (f32[8,1280]{1,0:T(8,128)S(1)}, f32[8,1280]{1,0:T(8,128)}, u32[]{:S(2)}) copy-start(f32[8,1280]{1,0:T(8,128)} %spread_ref.3) | copy-start | bytes 122884

commit v6 on v5

--- a/solution.py
+++ b/solution.py
@@ -122,7 +122,7 @@
     devices, owned = cols_ref.shape
     factor = math.sqrt(2.0 / points)
     lane = iota((1, 128), 1).astype(F32)
-    size = 64
+    size = 32
 
     def body(chunk, carry):
         start = pl.multiple_of(chunk * size, size)

time: 133 us -> 133 us (level)
  no operation moved by 1% of the time
where the time goes in v6:
time: 133 us
  blocking collectives  113 us (85%)
  Pallas kernels  17.7 us (13%)
    all_to_all x5, blocking collectives, exchange(): lax.all_to_all(buffer, ('lat', 'lev'), split_axis=0, concat_axis=0, tiled...  113 us
    pallas_call x2, Pallas kernels, spectral(): pl.pallas_call(functools.partial(spectral_kernel, rows, with_base), in_sp...  7.7 us
    pallas_call x1, Pallas kernels, local(): pl.pallas_call(first_kernel, in_specs=[SMEM, VMEM, HBM, HBM, HBM, HBM], o...  4.09 us
    pallas_call x1, Pallas kernels, local(): pl.pallas_call(middle_kernel, in_specs=[SMEM, VMEM, VMEM, VMEM, VMEM], ou...  3.26 us

profile of v6, /device:TPU:1, one launch (start us, length us, event | category | flops | bytes accessed | tf_op | source)
XLA Modules:
  0.0 132.6 jit_solution(15000742428046464257)
XLA Ops:
  0.6 0.0 copy-start.1
  0.6 0.0 copy-start
  0.7 0.9 reshape.33.cols_ref
  1.6 4.1 %first.1 = (bf16[2560,640]{1,0:T(8,128)(2,1)S(1)}, f32[256,128]{1,0:T(8,128)S(1)}, bf16[5,640,1280]{2,1,0:T(8,128)(2,1)S(1)}, f32[40,2560]{1,0:T(8,128)S(1)}, bf16[1024,128]{1,0:T(8,128)(2,1)S(1)}) custom-call(s32[1]{0:T(128)} %bitcast.owner_ref, s32[256,5]{1,0:T(8,128)S(1)} %reshape.33.cols_ref, f32[40,2560]{1,0:T(8,128)} %bitcast.27, s32[40,2560]{1,0:T(8,128)} %bitcast.28, ...), custom_call_target="tpu_custom_call" | custom-call | tf_op jit(solution)/shard_map/first/pallas_call | solution.py:413
  5.7 31.4 %all_to_all.55 = bf16[256,4,128]{2,1,0:T(4,128)(2,1)S(1)} all-to-all(bf16[256,4,128]{2,1,0:T(4,128)(2,1)S(1)} %bitcast.22), channel_id=1, replica_groups=mesh['lat'=32,'lev'=8] {'lat','lev'}, dimensions={0} | all-to-all | bytes 524288 | tf_op jit(solution)/shard_map/all_to_all | solution.py:396
  37.1 0.0 copy-done.1
  37.1 0.0 copy-done
  37.1 4.1 %spectral.2 = (f32[5,16,1280]{2,1,0:T(8,128)S(1)}, bf16[1024,128]{1,0:T(8,128)(2,1)S(1)}, bf16[5,1280,640]{2,1,0:T(8,128)(2,1)S(1)}) custom-call(s32[1]{0:T(128)} %bitcast.owner_ref, s32[1280]{0:T(1024)S(1)} %copy-done.1, bf16[1024,128]{1,0:T(8,128)(2,1)S(1)} %bitcast.19, bf16[5,640,1280]{2,1,0:T(8,128)(2,1)S(1)} %get-tuple-element.22.basis_ref, ...), custom_call_target="tpu_custom_call" | custom-call | tf_op jit(solution)/shard_map/spectral/pallas_call | solution.py:433
  41.1 21.1 %all_to_all.56 = bf16[256,4,128]{2,1,0:T(4,128)(2,1)S(1)} all-to-all(bf16[256,4,128]{2,1,0:T(4,128)(2,1)S(1)} %bitcast.24), channel_id=1, replica_groups=mesh['lat'=32,'lev'=8] {'lat','lev'}, dimensions={0} | all-to-all | bytes 524288 | tf_op jit(solution)/shard_map/all_to_all | solution.py:396
  62.3 3.3 %middle.1 = (f32[40,2560]{1,0:T(8,128)S(1)}, bf16[1024,128]{1,0:T(8,128)(2,1)S(1)}, f32[8,128]{1,0:T(8,128)S(1)}) custom-call(s32[1]{0:T(128)} %bitcast.owner_ref, bf16[1024,128]{1,0:T(8,128)(2,1)S(1)} %bitcast.18, bf16[2560,640]{1,0:T(8,128)(2,1)S(1)} %get-tuple-element.24.table_ref, f32[256,128]{1,0:T(8,128)S(1)} %get-tuple-element.25.turn_ref, ...), custom_call_target="tpu_custom_call" | custom-call | tf_op jit(solution)/shard_map/middle/pallas_call | solution.py:446
  65.6 21.3 %all_to_all.57 = bf16[256,4,128]{2,1,0:T(4,128)(2,1)S(1)} all-to-all(bf16[256,4,128]{2,1,0:T(4,128)(2,1)S(1)} %bitcast.25), channel_id=1, replica_groups=mesh['lat'=32,'lev'=8] {'lat','lev'}, dimensions={0} | all-to-all | bytes 524288 | tf_op jit(solution)/shard_map/all_to_all | solution.py:396
  86.9 3.6 %spectral.3 = (f32[5,16,1280]{2,1,0:T(8,128)S(1)}, bf16[1024,128]{1,0:T(8,128)(2,1)S(1)}, f32[8,128]{1,0:T(8,128)S(1)}) custom-call(s32[1]{0:T(128)} %bitcast.owner_ref, s32[1280]{0:T(1024)S(1)} %copy-done.1, bf16[1024,128]{1,0:T(8,128)(2,1)S(1)} %bitcast.17, bf16[5,640,1280]{2,1,0:T(8,128)(2,1)S(1)} %get-tuple-element.22.basis_ref, f32[8,1280]{1,0:T(8,128)S(1)} %copy-done, ...), custom_call_target="tpu_custom_call" | custom-call | tf_op jit(solution)/shard_map/spectral/pallas_call | solution.py:433
  90.5 21.1 %all_to_all.58 = bf16[256,4,128]{2,1,0:T(4,128)(2,1)S(1)} all-to-all(bf16[256,4,128]{2,1,0:T(4,128)(2,1)S(1)} %bitcast.23), channel_id=1, replica_groups=mesh['lat'=32,'lev'=8] {'lat','lev'}, dimensions={0} | all-to-all | bytes 524288 | tf_op jit(solution)/shard_map/all_to_all | solution.py:396
  111.6 1.6 %last.1 = (f32[40,2560]{1,0:T(8,128)S(1)}, f32[256,128]{1,0:T(8,128)S(1)}, f32[8,128]{1,0:T(8,128)S(1)}) custom-call(s32[1]{0:T(128)} %bitcast.owner_ref, bf16[1024,128]{1,0:T(8,128)(2,1)S(1)} %bitcast.20, bf16[2560,640]{1,0:T(8,128)(2,1)S(1)} %get-tuple-element.24.table_ref, f32[256,128]{1,0:T(8,128)S(1)} %get-tuple-element.25.turn_ref, ...), custom_call_target="tpu_custom_call" | custom-call | tf_op jit(solution)/shard_map/last/pallas_call | solution.py:456
  113.3 18.3 %all_to_all.59 = f32[256,1,128]{2,1,0:T(1,128)S(1)} all-to-all(f32[256,1,128]{2,1,0:T(1,128)S(1)} %bitcast.26), channel_id=1, replica_groups=mesh['lat'=32,'lev'=8] {'lat','lev'}, dimensions={0} | all-to-all | bytes 262144 | tf_op jit(solution)/shard_map/all_to_all | solution.py:396
  131.5 1.0 finish.1
Async XLA Ops:
  0.6 36.4 %copy-start.1 = (s32[1280]{0:T(1024)S(1)}, s32[1280]{0:T(1024)}, u32[]{:S(2)}) copy-start(s32[1280]{0:T(1024)} %order_ref.3) | copy-start | bytes 15364
  0.6 36.4 %copy-start = (f32[8,1280]{1,0:T(8,128)S(1)}, f32[8,1280]{1,0:T(8,128)}, u32[]{:S(2)}) copy-start(f32[8,1280]{1,0:T(8,128)} %spread_ref.3) | copy-start | bytes 122884
